TPU v7x, 128 devices: a whole 4x4x4 slice. The times are simulated.
128 devices in a mesh: row: 16 (over x, z_hi, core), col: 8 (over z_lo, y).
Axes of the slice: x: 4, y: 4, z: 4 (z_hi: 2, z_lo: 2; z = z_hi * 2 + z_lo), core: 2. Of those that a mesh axis runs over, the one named last changes fastest.
Arguments:
- pair_rep: bfloat16 [512, 512, 128], P('row', 'col'), may hold values from -6 to 6
- w_proj: bfloat16 [2, 128, 512], replicated, may hold values from -0.5 to 0.5
- w_gate: bfloat16 [2, 128, 128], replicated, may hold values from -0.5 to 0.5
- w_out: bfloat16 [2, 128, 128], replicated, may hold values from -0.5 to 0.5
- norm_gain: float32 [2, 2, 128], replicated, may hold values from 0.5 to 1.5
- norm_shift: float32 [2, 2, 128], replicated, may hold values from -0.6 to 0.6
Outputs:
- new_pair: bfloat16 [512, 512, 128], P('row', 'col')
All inputs are finite; a program needn't handle non-finite values.
Results may differ from a plain program's by a relative error of at most 0.023.
Values may be sent and summed in bfloat16 or wider, within the bound.
A program may use at most 128 MiB of HBM per device.

v0:
```python
import jax
import jax.numpy as jnp
from jax import lax
from jax.sharding import PartitionSpec as P

EPSILON = 1e-05


def layer_norm(values, gain, shift):
    average = jnp.mean(values, axis=-1, keepdims=True)
    centred = values - average
    variance = jnp.mean(centred * centred, axis=-1, keepdims=True)
    return centred * lax.rsqrt(variance + EPSILON) * gain + shift


def project(pair_rep, proj_weight, gate_weight, gain, shift):
    hidden = proj_weight.shape[1] // 4
    normed = layer_norm(pair_rep.astype(jnp.float32), gain[0], shift[0]).astype(jnp.bfloat16)
    mixed = jnp.dot(normed, proj_weight, preferred_element_type=jnp.float32)
    left_proj = (jax.nn.sigmoid(mixed[..., 0:hidden]) * mixed[..., hidden : 2 * hidden]).astype(
        jnp.bfloat16
    )
    right_proj = (
        jax.nn.sigmoid(mixed[..., 2 * hidden : 3 * hidden]) * mixed[..., 3 * hidden : 4 * hidden]
    ).astype(jnp.bfloat16)
    gating = jax.nn.sigmoid(jnp.dot(normed, gate_weight, preferred_element_type=jnp.float32))
    return (left_proj, right_proj, gating)


def finish(pair_rep, summed, gating, out_weight, gain, shift):
    normed = layer_norm(summed, gain[1], shift[1]).astype(jnp.bfloat16)
    branch = jnp.dot(normed, out_weight, preferred_element_type=jnp.float32)
    return (pair_rep.astype(jnp.float32) + gating * branch).astype(jnp.bfloat16)


def body(pair_rep, w_proj, w_gate, w_out, norm_gain, norm_shift):
    left_proj, right_proj, gating = project(
        pair_rep, w_proj[0], w_gate[0], norm_gain[0], norm_shift[0]
    )
    partial_sums = jnp.einsum(
        "ikc,jkc->ijc",
        left_proj,
        lax.all_gather(right_proj, "row", axis=0, tiled=True),
        preferred_element_type=jnp.float32,
    )
    summed = lax.psum_scatter(
        partial_sums.astype(jnp.bfloat16), "col", scatter_dimension=1, tiled=True
    ).astype(jnp.float32)
    updated = finish(pair_rep, summed, gating, w_out[0], norm_gain[0], norm_shift[0])
    left_proj, right_proj, gating = project(
        updated, w_proj[1], w_gate[1], norm_gain[1], norm_shift[1]
    )
    partial_sums = jnp.einsum(
        "kic,kjc->ijc",
        lax.all_gather(left_proj, "col", axis=1, tiled=True),
        right_proj,
        preferred_element_type=jnp.float32,
    )
    summed = lax.psum_scatter(
        partial_sums.astype(jnp.bfloat16), "row", scatter_dimension=0, tiled=True
    ).astype(jnp.float32)
    return finish(updated, summed, gating, w_out[1], norm_gain[1], norm_shift[1])


def solution(mesh):
    in_specs = (P("row", "col", None), P(), P(), P(), P(), P())
    out_specs = P("row", "col", None)
    return jax.shard_map(body, mesh=mesh, in_specs=in_specs, out_specs=out_specs, check_vma=False)
```

profile of v0, /device:TPU:1, one launch (start us, length us, event | category | flops | bytes accessed | tf_op | source)
XLA Modules:
  0.0 388.1 jit_solution(5136982076116044880)
XLA Ops:
  6.5 1.4 convert_reduce_fusion.1
  7.9 1.7 fusion.22
  10.4 2.0 fusion.50
  12.5 1.3 fusion.42
  13.9 1.6 copy.44
  15.5 74.8 %all-gather.3.cloned.1.call-done = bf16[512,64,128]{2,1,0:T(8,128)(2,1)} async-done(((bf16[32,64,128]{2,1,0:T(8,128)(2,1)}), bf16[512,64,128]{2,1,0:T(8,128)(2,1)}) %all-gather.3.cloned.1.call-update) | async-done | bytes 8388624 | tf_op jit(solution)/shard_map/all_gather | solution.py:43
  90.4 23.7 %copy.43 = bf16[512,64,128]{1,0,2:T(8,128)(2,1)} copy(bf16[512,64,128]{2,1,0:T(8,128)(2,1)} %all-gather.3.cloned.1.call-done) | data formatting | bytes 16777216 | tf_op jit(solution)/shard_map/all_gather | solution.py:43
  114.1 10.7 %convert_bitcast_fusion.1 = bf16[32,512,128]{1,0,2:T(8,128)(2,1)} fusion(bf16[512,64,128]{1,0,2:T(8,128)(2,1)} %copy.43, bf16[32,64,128]{1,0,2:T(8,128)(2,1)S(1)} %copy.44), kind=kOutput, calls=%fused_computation.1 | convolution fusion | flops 270532608 | bytes 13107200 | tf_op jit(solution)/shard_map/ikc,jkc->ijc/dot_general | solution.py:40
  124.8 9.1 %copy.45 = bf16[32,512,128]{2,0,1:T(8,128)(2,1)} copy(bf16[32,512,128]{1,0,2:T(8,128)(2,1)} %convert_bitcast_fusion.1) | data formatting | bytes 8388608 | tf_op jit(solution)/shard_map/convert_element_type | solution.py:47
  134.0 50.6 %reduce-scatter.3.cloned.1.call-done = bf16[32,64,128]{2,0,1:T(8,128)(2,1)} async-done(((bf16[32,512,128]{2,0,1:T(8,128)(2,1)}), bf16[32,64,128]{2,0,1:T(8,128)(2,1)}) %reduce-scatter.3.cloned.1.call-update) | async-done | bytes 524304 | tf_op jit(solution)/shard_map/reduce_scatter | solution.py:46
  184.6 1.4 convert_reduce_fusion.3
  186.1 1.7 fusion.30
  188.0 1.7 fusion.33
  192.6 1.3 fusion.34
  194.2 1.6 copy.51
  195.8 49.6 %all-gather.5.cloned.1.call-done = bf16[32,512,128]{2,1,0:T(8,128)(2,1)} async-done(((bf16[32,64,128]{2,1,0:T(8,128)(2,1)}), bf16[32,512,128]{2,1,0:T(8,128)(2,1)}) %all-gather.5.cloned.1.call-update) | async-done | bytes 4194320 | tf_op jit(solution)/shard_map/all_gather | solution.py:55
  245.5 7.9 %copy.52 = bf16[32,512,128]{1,0,2:T(8,128)(2,1)} copy(bf16[32,512,128]{2,1,0:T(8,128)(2,1)} %all-gather.5.cloned.1.call-done) | data formatting | bytes 8388608 | tf_op jit(solution)/shard_map/all_gather | solution.py:55
  253.4 7.8 %convert_bitcast_fusion = bf16[512,64,128]{0,1,2:T(8,128)(2,1)} fusion(bf16[32,64,128]{1,0,2:T(8,128)(2,1)S(1)} %copy.51, bf16[32,512,128]{1,0,2:T(8,128)(2,1)} %copy.52), kind=kOutput, calls=%fused_computation | convolution fusion | flops 272629760 | bytes 13107200 | tf_op jit(solution)/shard_map/kic,kjc->ijc/dot_general | solution.py:53
  261.1 13.7 %copy.53 = bf16[512,64,128]{2,1,0:T(8,128)(2,1)} copy(bf16[512,64,128]{0,1,2:T(8,128)(2,1)} %convert_bitcast_fusion) | data formatting | bytes 16777216 | tf_op jit(solution)/shard_map/convert_element_type | solution.py:60
  274.8 100.2 %reduce-scatter.5.cloned.1.call-done = bf16[32,64,128]{2,1,0:T(8,128)(2,1)} async-done(((bf16[512,64,128]{2,1,0:T(8,128)(2,1)}), bf16[32,64,128]{2,1,0:T(8,128)(2,1)}) %reduce-scatter.5.cloned.1.call-update) | async-done | bytes 524304 | tf_op jit(solution)/shard_map/reduce_scatter | solution.py:59
  375.0 1.4 convert_reduce_fusion.2
  376.4 1.7 fusion.26
  378.1 1.8 fusion.56
  379.9 1.7 fusion.9
  (33 shorter events, 4.4 us)
Async XLA Ops:
  6.5 83.8 %all-gather.3.cloned.1.call-start = ((), (), s32[]{:S(2)}) async-start(), calls=%async_computation.2 | async-start | bytes 8912896 | tf_op jit(solution)/shard_map/all_gather | solution.py:43
  13.8 170.7 %reduce-scatter.3.cloned.1.call-start = ((), (), s32[]{:S(2)}) async-start(), calls=%async_computation.3 | async-start | bytes 4718592 | tf_op jit(solution)/shard_map/reduce_scatter | solution.py:46
  133.9 55.7 %copy-start.2 = (bf16[2,128,128]{2,1,0:T(8,128)(2,1)S(1)}, bf16[2,128,128]{2,1,0:T(8,128)(2,1)}, u32[]{:S(2)}) copy-start(bf16[2,128,128]{2,1,0:T(8,128)(2,1)} %param.9) | copy-start | bytes 196612
  133.9 56.0 %copy-start = (bf16[32,64,128]{2,1,0:T(8,128)(2,1)S(1)}, bf16[32,64,128]{2,1,0:T(8,128)(2,1)}, u32[]{:S(2)}) copy-start(bf16[32,64,128]{2,1,0:T(8,128)(2,1)} %param.6) | copy-start | bytes 1572868
  133.9 56.0 %copy-start.3 = (bf16[2,128,128]{2,1,0:T(8,128)(2,1)S(1)}, bf16[2,128,128]{2,1,0:T(8,128)(2,1)}, u32[]{:S(2)}) copy-start(bf16[2,128,128]{2,1,0:T(8,128)(2,1)} %param.8) | copy-start | bytes 196612
  133.9 111.5 %all-gather.5.cloned.1.call-start = ((), (), s32[]{:S(2)}) async-start(), calls=%async_computation.4 | async-start | bytes 4718592 | tf_op jit(solution)/shard_map/all_gather | solution.py:55
  189.6 2.2 copy-start.1
  194.0 181.0 %reduce-scatter.5.cloned.1.call-start = ((), (), s32[]{:S(2)}) async-start(), calls=%async_computation.5 | async-start | bytes 8912896 | tf_op jit(solution)/shard_map/reduce_scatter | solution.py:59
Sparse Core Ops, SparseCore 0:
  13.9 76.3 all-gather.2
  134.1 50.4 reduce-scatter.2
  194.1 51.3 all-gather.4
  275.0 100.0 reduce-scatter.4
where the time goes:
time: 390 us; the launch traced here: 388 us
  waiting for transfers between devices  275 us (71%)
  local copies, waits for them, and re-layouts  58.8 us (15%)
  matrix products  26.2 us (7%)
  other arithmetic  14.3 us (4%)
  between operations  13.3 us (3%)
    reduce_scatter x1, waiting for transfers between devices, body(): lax.psum_scatter(partial_sums.astype(jnp.bfloat16), 'row', scatter_dimens...  100 us
    all_gather x1, waiting for transfers between devices, body(): lax.all_gather(right_proj, 'row', axis=0, tiled=True)  74.8 us
    reduce_scatter x1, waiting for transfers between devices, body(): lax.psum_scatter(partial_sums.astype(jnp.bfloat16), 'col', scatter_dimens...  50.6 us
    all_gather x1, waiting for transfers between devices, body(): lax.all_gather(left_proj, 'col', axis=1, tiled=True)  49.6 us
    all_gather x1, local copies, waits for them, and re-layouts, body(): lax.all_gather(right_proj, 'row', axis=0, tiled=True)  23.7 us
    convert_element_type x2, local copies, waits for them, and re-layouts, body(): partial_sums.astype(jnp.bfloat16)  22.8 us
    dot_general x1, matrix products, body(): jnp.einsum('ikc,jkc->ijc', left_proj, lax.all_gather(right_proj, 'row', a...  10.7 us
    all_gather x1, local copies, waits for them, and re-layouts, body(): lax.all_gather(left_proj, 'col', axis=1, tiled=True)  7.89 us
  transfers between devices with their start and end apart: 4, of which 4 were waited for; matrix products, arithmetic and copies ran while one was open for 1% of the time, Pallas kernels for 0%

commit v1 on v0

v1 whole, which is shorter than its diff:
```python
import functools

import jax
import jax.numpy as jnp
from jax import lax
from jax.experimental import pallas as pl
from jax.experimental.pallas import tpu as pltpu
from jax.sharding import PartitionSpec as P

MESH = pl.DeviceIdType.MESH
EPSILON = 1e-05
C = 128
RES = 512
LANES = 128
TILE = 16
HALF = 64


def sigmoid(x):
    return 0.5 * jnp.tanh(0.5 * x) + 0.5


def norm(values, gain, shift):
    average = jnp.sum(values, axis=0, keepdims=True) * (1.0 / C)
    centred = values - average
    variance = jnp.sum(centred * centred, axis=0, keepdims=True) * (1.0 / C)
    return centred * lax.rsqrt(variance + EPSILON) * gain + shift


def swap(first, second):
    return (
        jnp.concatenate([first[:, :HALF], second[:, :HALF]], axis=1),
        jnp.concatenate([first[:, HALF:], second[:, HALF:]], axis=1),
    )


def kernel(
    rows, cols, pair, w_proj, w_gate, w_out, gain, shift, out,
    w_in_t, w_out_t, gain_t, shift_t, pair_t, gate_t, left_f, right_f,
    send, recv, ssend, srecv, left_m, right_m,
    send_sem, recv_sem, own_sem, ssend_sem, srecv_sem, sown_sem,
):
    devices = rows * cols
    me = lax.axis_index("row") * cols + lax.axis_index("col")

    def place(device):
        return (device // cols, lax.rem(device, cols))

    barrier = pltpu.get_barrier_semaphore()

    def greet(t, _):
        pl.semaphore_signal(
            barrier, inc=1, device_id=place(lax.rem(me + t, devices)), device_id_type=MESH
        )
        return 0

    lax.fori_loop(1, devices, greet, 0)

    for u in range(2):
        w_in_t[u, : 4 * C, :] = w_proj[u].astype(jnp.float32).T.astype(jnp.bfloat16)
        w_in_t[u, 4 * C :, :] = w_gate[u].astype(jnp.float32).T.astype(jnp.bfloat16)
        w_out_t[u] = w_out[u].astype(jnp.float32).T.astype(jnp.bfloat16)
        for n in range(2):
            gain_t[u, n] = jnp.broadcast_to(gain[u, n : n + 1, :], (C, LANES)).T
            shift_t[u, n] = jnp.broadcast_to(shift[u, n : n + 1, :], (C, LANES)).T

    def project(u, s, values):
        normed = norm(values, gain_t[u, 0], shift_t[u, 0]).astype(jnp.bfloat16)
        mixed = jnp.dot(w_in_t[u], normed, preferred_element_type=jnp.float32)
        left_f[pl.ds(s, C, stride=TILE), :] = sigmoid(mixed[:C]) * mixed[C : 2 * C]
        right_f[pl.ds(s, C, stride=TILE), :] = sigmoid(mixed[2 * C : 3 * C]) * mixed[3 * C : 4 * C]
        gate_t[s] = sigmoid(mixed[4 * C :])
        pair_t[s] = values

    def pack(u):
        group = 8

        def step(g, _):
            for side, source in ((0, left_f), (1, right_f)):
                block = source[pl.ds(pl.multiple_of(g * group * TILE, group * TILE), group * TILE), :]
                send[u, pl.ds(g * group, group), side] = block.reshape(group, TILE, LANES).astype(jnp.bfloat16)
            return 0

        lax.fori_loop(0, C // group, step, 0)

    def exchange(u):
        def step(t, _):
            d = lax.rem(me + t, devices)
            pltpu.make_async_remote_copy(
                src_ref=send.at[u, d], dst_ref=recv.at[u, me],
                send_sem=send_sem.at[u], recv_sem=recv_sem.at[u],
                device_id=place(d), device_id_type=MESH,
            ).start()
            return 0

        own = pltpu.make_async_copy(send.at[u, me], recv.at[u, me], own_sem.at[u])
        own.start()
        lax.fori_loop(1, devices, step, 0)
        own.wait()
        some = pl.ds(0, devices - 1)
        pltpu.make_async_copy(recv.at[u, some], recv.at[u, some], recv_sem.at[u]).wait()

    def gather(u):
        def step(r, _):
            for m in range(cols // 2):
                for side, matrix in ((0, left_m), (1, right_m)):
                    upper, lower = swap(recv[u, r * cols + 2 * m, side], recv[u, r * cols + 2 * m + 1, side])
                    top = pl.multiple_of(r * 2 * TILE, 2 * TILE)
                    matrix[pl.ds(top, TILE), m * LANES : (m + 1) * LANES] = upper
                    matrix[pl.ds(top + TILE, TILE), m * LANES : (m + 1) * LANES] = lower
            return 0

        lax.fori_loop(0, rows, step, 0)

    def product(u):
        if u == 0:
            dims = (((1,), (1,)), ((), ()))
        else:
            dims = (((1,), (0,)), ((), ()))
            left_m[...] = left_m[...].astype(jnp.float32).T.astype(jnp.bfloat16)
        group = 4
        first = lax.axis_index("row") // group

        def step(b, _):
            block = lax.rem(first + b, rows // group)
            height = group * 2 * TILE
            left = left_m[pl.ds(pl.multiple_of(block * height, height), height), :]
            sums = lax.dot_general(left, right_m[...], dims, preferred_element_type=jnp.float32)
            sums = sums.astype(jnp.bfloat16)
            for k in range(group):
                for m in range(cols // 2):
                    columns = slice(m * LANES, (m + 1) * LANES)
                    a, b_ = swap(
                        sums[k * 2 * TILE : k * 2 * TILE + TILE, columns],
                        sums[k * 2 * TILE + TILE : (k + 1) * 2 * TILE, columns],
                    )
                    d = (block * group + k) * cols + 2 * m
                    ssend[u, d] = a
                    ssend[u, d + 1] = b_

            def out_step(t, _):
                d = block * group * cols + lax.rem(t + me, group * cols)

                @pl.when(d != me)
                def _():
                    pltpu.make_async_remote_copy(
                        src_ref=ssend.at[u, d], dst_ref=srecv.at[u, me],
                        send_sem=ssend_sem.at[u], recv_sem=srecv_sem.at[u],
                        device_id=place(d), device_id_type=MESH,
                    ).start()

                return 0

            lax.fori_loop(0, group * cols, out_step, 0)
            return 0

        lax.fori_loop(0, rows // group, step, 0)
        own = pltpu.make_async_copy(ssend.at[u, me], srecv.at[u, me], sown_sem.at[u])
        own.start()
        own.wait()
        some = pl.ds(0, devices - 1)
        pltpu.make_async_copy(srecv.at[u, some], srecv.at[u, some], srecv_sem.at[u]).wait()

    def widen(u):
        group = 8

        def step(g, _):
            block = srecv[u, pl.ds(g * group, group)].astype(jnp.float32).reshape(group * TILE, LANES)
            left_f[pl.ds(pl.multiple_of(g * group * TILE, group * TILE), group * TILE), :] = block
            return 0

        lax.fori_loop(0, C // group, step, 0)

    def finish(u, s):
        sums = left_f[pl.ds(s, C, stride=TILE), :]
        normed = norm(sums, gain_t[u, 1], shift_t[u, 1]).astype(jnp.bfloat16)
        branch = jnp.dot(w_out_t[u], normed, preferred_element_type=jnp.float32)
        return (pair_t[s] + gate_t[s] * branch).astype(jnp.bfloat16).astype(jnp.float32)

    def first_step(s, _):
        values = jnp.concatenate([pair[s], pair[s + TILE]], axis=0)
        project(0, s, values.astype(jnp.float32).T)
        return 0

    lax.fori_loop(0, TILE, first_step, 0)
    pack(0)
    pl.semaphore_wait(barrier, devices - 1)
    exchange(0)
    gather(0)
    product(0)
    widen(0)

    def second_step(s, _):
        project(1, s, finish(0, s))
        return 0

    lax.fori_loop(0, TILE, second_step, 0)
    pack(1)
    exchange(1)
    gather(1)
    product(1)
    widen(1)

    def last_step(s, _):
        values = finish(1, s).T.astype(jnp.bfloat16)
        out[s] = values[:HALF]
        out[s + TILE] = values[HALF:]
        return 0

    lax.fori_loop(0, TILE, last_step, 0)
    some = pl.ds(0, devices - 1)
    for u in range(2):
        pltpu.make_async_copy(send.at[u, some], send.at[u, some], send_sem.at[u]).wait()
        pltpu.make_async_copy(ssend.at[u, some], ssend.at[u, some], ssend_sem.at[u]).wait()


def solution(mesh):
    rows, cols = mesh.shape["row"], mesh.shape["col"]
    devices = rows * cols
    bf16, f32 = jnp.bfloat16, jnp.float32
    vmem = pl.BlockSpec(memory_space=pltpu.VMEM)

    def body(pair_rep, w_proj, w_gate, w_out, norm_gain, norm_shift):
        return pl.pallas_call(
            functools.partial(kernel, rows, cols),
            out_shape=jax.ShapeDtypeStruct(pair_rep.shape, bf16),
            in_specs=[vmem] * 6,
            out_specs=vmem,
            scratch_shapes=[
                pltpu.VMEM((2, 5 * C, C), bf16),
                pltpu.VMEM((2, C, C), bf16),
                pltpu.VMEM((2, 2, C, LANES), f32),
                pltpu.VMEM((2, 2, C, LANES), f32),
                pltpu.VMEM((TILE, C, LANES), f32),
                pltpu.VMEM((TILE, C, LANES), f32),
                pltpu.VMEM((C * TILE, LANES), f32),
                pltpu.VMEM((C * TILE, LANES), f32),
                pltpu.VMEM((2, devices, 2, TILE, LANES), bf16),
                pltpu.VMEM((2, devices, 2, TILE, LANES), bf16),
                pltpu.VMEM((2, devices, TILE, LANES), bf16),
                pltpu.VMEM((2, devices, TILE, LANES), bf16),
                pltpu.VMEM((RES, RES), bf16),
                pltpu.VMEM((RES, RES), bf16),
            ]
            + [pltpu.SemaphoreType.DMA((2,))] * 6,
            compiler_params=pltpu.CompilerParams(
                collective_id=0, has_side_effects=True, vmem_limit_bytes=48 << 20
            ),
        )(pair_rep, w_proj, w_gate, w_out, norm_gain, norm_shift)

    in_specs = (P("row", "col", None), P(), P(), P(), P(), P())
    return jax.shard_map(
        body, mesh=mesh, in_specs=in_specs, out_specs=P("row", "col", None), check_vma=False
    )
```

time: 390 us -> 94.2 us (0.24)
  waiting for transfers between devices: 275 us -> 0 us
  Pallas kernels: 0 us -> 88 us
  local copies, waits for them, and re-layouts: 58.8 us -> 5.83 us
  matrix products: 26.2 us -> 0 us
  other arithmetic: 14.3 us -> 0 us
  between operations: 13.3 us -> 0.02 us
    reduce_scatter x2 -> x0, waiting for transfers between devices: 151 us -> none  [the longest x1 100 us: body(): lax.psum_scatter(partial_sums.astype(jnp.bfloat16), 'row', scatter_dimens...]
    all_gather x2 -> x0, waiting for transfers between devices: 124 us -> none  [the longest x1 74.8 us: body(): lax.all_gather(right_proj, 'row', axis=0, tiled=True)]
    pallas_call x0 -> x1, Pallas kernels: none -> 88 us  [body(): pl.pallas_call(functools.partial(kernel, rows, cols), out_shape=jax.Shape...]
    all_gather x2 -> x0, local copies, waits for them, and re-layouts: 31.6 us -> none  [the longest x1 23.7 us: body(): lax.all_gather(right_proj, 'row', axis=0, tiled=True)]
    dot_general x8 -> x0, matrix products: 26.2 us -> none  [the longest x1 10.7 us: body(): jnp.einsum('ikc,jkc->ijc', left_proj, lax.all_gather(right_proj, 'row', a...]
    convert_element_type x4 -> x0, local copies, waits for them, and re-layouts: 26 us -> none  [the longest x2 22.8 us: body(): partial_sums.astype(jnp.bfloat16)]
    reduce_sum x7 -> x0, other arithmetic: 9.85 us -> none  [the longest x4 5.7 us: layer_norm(): variance = jnp.mean(centred * centred, axis=-1, keepdims=True)]
    unnamed x8 -> x13, local copies, waits for them, and re-layouts: 0.02 us -> 5.83 us
  transfers between devices with their start and end apart: 4 -> 0, of which waited for: 4 -> 0; matrix products, arithmetic and copies ran while one was open for 1% -> 0% of each run, Pallas kernels for 0% -> 0%
where the time goes in v1:
time: 94.2 us; the launch traced here: 93.9 us
  Pallas kernels  88 us (93%)
  local copies, waits for them, and re-layouts  5.83 us (6%)
    pallas_call x1, Pallas kernels, body(): pl.pallas_call(functools.partial(kernel, rows, cols), out_shape=jax.Shape...  88 us
    unnamed x13, local copies, waits for them, and re-layouts  5.83 us

profile of v1, /device:TPU:1, one launch (start us, length us, event | category | flops | bytes accessed | tf_op | source)
XLA Modules:
  0.0 93.9 jit_solution(13680972018497327457)
XLA Ops:
  0.0 0.0 copy-start
  0.0 1.0 %copy-done = bf16[32,64,128]{2,1,0:T(8,128)(2,1)S(1)} copy-done((bf16[32,64,128]{2,1,0:T(8,128)(2,1)S(1)}, bf16[32,64,128]{2,1,0:T(8,128)(2,1)}, u32[]{:S(2)}) %copy-start) | copy-done | bytes 524312
  1.0 0.0 copy-start.1
  1.0 0.9 %copy-done.1 = bf16[2,128,512]{2,1,0:T(8,128)(2,1)S(1)} copy-done((bf16[2,128,512]{2,1,0:T(8,128)(2,1)S(1)}, bf16[2,128,512]{2,1,0:T(8,128)(2,1)}, u32[]{:S(2)}) %copy-start.1) | copy-done | bytes 262168
  2.0 0.0 copy-start.2
  2.0 0.8 copy-done.2
  2.8 0.0 copy-start.3
  2.8 0.8 copy-done.3
  3.7 0.0 copy-start.4
  3.7 0.7 copy-done.4
  4.4 0.0 copy-start.5
  4.4 0.7 copy-done.5
  5.0 88.0 %shard_map.64 = bf16[32,64,128]{2,1,0:T(8,128)(2,1)S(1)} custom-call(bf16[32,64,128]{2,1,0:T(8,128)(2,1)S(1)} %copy-done, bf16[2,128,512]{2,1,0:T(8,128)(2,1)S(1)} %copy-done.1, bf16[2,128,128]{2,1,0:T(8,128)(2,1)S(1)} %copy-done.2, bf16[2,128,128]{2,1,0:T(8,128)(2,1)S(1)} %copy-done.3, f32[2,2,128]{2,1,0:T(2,128)S(1)} %copy-done.4, f32[2,2,128]{2,1,0:T(2,128)S(1)} %copy-done.5), custom_call_target="tpu_custom_call" | custom-call | tf_op jit(solution)/shard_map/pallas_call | solution.py:224
  93.1 0.8 copy.8
Async XLA Ops:
  0.0 1.0 %copy-start = (bf16[32,64,128]{2,1,0:T(8,128)(2,1)S(1)}, bf16[32,64,128]{2,1,0:T(8,128)(2,1)}, u32[]{:S(2)}) copy-start(bf16[32,64,128]{2,1,0:T(8,128)(2,1)} %pair.1) | copy-start | bytes 1572868
  1.0 0.9 %copy-start.1 = (bf16[2,128,512]{2,1,0:T(8,128)(2,1)S(1)}, bf16[2,128,512]{2,1,0:T(8,128)(2,1)}, u32[]{:S(2)}) copy-start(bf16[2,128,512]{2,1,0:T(8,128)(2,1)} %w_proj.1) | copy-start | bytes 786436
  2.0 0.8 copy-start.2
  2.8 0.8 copy-start.3
  3.7 0.7 copy-start.4
  4.4 0.7 copy-start.5

commit v2 on v1

--- a/solution.py
+++ b/solution.py
@@ -13,11 +13,20 @@
 RES = 512
 LANES = 128
 TILE = 16
+WIDE = 4
 HALF = 64
 
 
 def sigmoid(x):
     return 0.5 * jnp.tanh(0.5 * x) + 0.5
+
+
+def far_first():
+    def hops(offset):
+        return sum(min(v, 4 - v) for v in (offset // 16, offset // 4 % 4, offset % 4))
+
+    order = sorted(range(64), key=lambda offset: -hops(offset))
+    return order
 
 
 def norm(values, gain, shift):
@@ -35,26 +44,70 @@
 
 
 def kernel(
-    rows, cols, pair, w_proj, w_gate, w_out, gain, shift, out,
+    rows, cols, pair_h, w_proj_h, w_gate_h, w_out_h, gain_h, shift_h, out,
+    pair, w_proj, w_gate, w_out, gain, shift,
     w_in_t, w_out_t, gain_t, shift_t, pair_t, gate_t, left_f, right_f,
     send, recv, ssend, srecv, left_m, right_m,
-    send_sem, recv_sem, own_sem, ssend_sem, srecv_sem, sown_sem,
+    send_sem, recv_sem, own_sem, ssend_sem, srecv_sem, sown_sem, in_sem, ready,
 ):
     devices = rows * cols
     me = lax.axis_index("row") * cols + lax.axis_index("col")
 
-    def place(device):
-        return (device // cols, lax.rem(device, cols))
-
+    loads = [
+        pltpu.make_async_copy(source, target, in_sem.at[k])
+        for k, (source, target) in enumerate((
+            (w_proj_h, w_proj), (w_gate_h, w_gate), (w_out_h, w_out),
+            (gain_h, gain), (shift_h, shift), (pair_h, pair),
+        ))
+    ]
+    for load in loads:
+        load.start()
+
+    row, col = lax.axis_index("row"), lax.axis_index("col")
     barrier = pltpu.get_barrier_semaphore()
 
-    def greet(t, _):
+    def greet_row(t, _):
         pl.semaphore_signal(
-            barrier, inc=1, device_id=place(lax.rem(me + t, devices)), device_id_type=MESH
+            barrier, inc=1, device_id=(lax.rem(row + t, rows), col), device_id_type=MESH
         )
         return 0
 
-    lax.fori_loop(1, devices, greet, 0)
+    def greet_col(semaphore):
+        def step(t, _):
+            pl.semaphore_signal(
+                semaphore, inc=1, device_id=(row, lax.rem(col + t, cols)), device_id_type=MESH
+            )
+            return 0
+
+        lax.fori_loop(1, cols, step, 0)
+
+    lax.fori_loop(1, rows, greet_row, 0)
+    greet_col(barrier)
+
+    x, y, z, core = row // 4, lax.rem(col, 4), lax.rem(row // 2, 2) * 2 + col // 4, lax.rem(row, 2)
+
+    def everyone(start):
+        order = far_first()
+        for flip, offsets in ((1, order), (0, order[:-1])):
+            for k in range(0, len(offsets), 5):
+                part = offsets[k : k + 5]
+                digits = sum(offset * 64**n for n, offset in enumerate(part))
+
+                def step(_, rest, flip=flip):
+                    offset = lax.rem(rest, 64)
+                    x_, y_, z_ = (
+                        lax.rem(x + offset // 16, 4),
+                        lax.rem(y + lax.rem(offset // 4, 4), 4),
+                        lax.rem(z + lax.rem(offset, 4), 4),
+                    )
+                    core_ = lax.rem(core + flip, 2)
+                    start(x_ * 4 + (z_ // 2) * 2 + core_, lax.rem(z_, 2) * 4 + y_)
+                    return rest // 64
+
+                lax.fori_loop(0, len(part), step, jnp.int32(digits))
+
+    for load in loads[:5]:
+        load.wait()
 
     for u in range(2):
         w_in_t[u, : 4 * C, :] = w_proj[u].astype(jnp.float32).T.astype(jnp.bfloat16)
@@ -64,13 +117,20 @@
             gain_t[u, n] = jnp.broadcast_to(gain[u, n : n + 1, :], (C, LANES)).T
             shift_t[u, n] = jnp.broadcast_to(shift[u, n : n + 1, :], (C, LANES)).T
 
+    def wide(block):
+        return jnp.concatenate([block] * WIDE, axis=1)
+
     def project(u, s, values):
-        normed = norm(values, gain_t[u, 0], shift_t[u, 0]).astype(jnp.bfloat16)
+        normed = norm(values, wide(gain_t[u, 0]), wide(shift_t[u, 0])).astype(jnp.bfloat16)
         mixed = jnp.dot(w_in_t[u], normed, preferred_element_type=jnp.float32)
-        left_f[pl.ds(s, C, stride=TILE), :] = sigmoid(mixed[:C]) * mixed[C : 2 * C]
-        right_f[pl.ds(s, C, stride=TILE), :] = sigmoid(mixed[2 * C : 3 * C]) * mixed[3 * C : 4 * C]
-        gate_t[s] = sigmoid(mixed[4 * C :])
-        pair_t[s] = values
+        left = sigmoid(mixed[:C]) * mixed[C : 2 * C]
+        right = sigmoid(mixed[2 * C : 3 * C]) * mixed[3 * C : 4 * C]
+        for k in range(WIDE):
+            lanes = slice(k * LANES, (k + 1) * LANES)
+            left_f[pl.ds(s + k, C, stride=TILE), :] = left[:, lanes]
+            right_f[pl.ds(s + k, C, stride=TILE), :] = right[:, lanes]
+        gate_t[s // WIDE] = sigmoid(mixed[4 * C :])
+        pair_t[s // WIDE] = values
 
     def pack(u):
         group = 8
@@ -84,18 +144,17 @@
         lax.fori_loop(0, C // group, step, 0)
 
     def exchange(u):
-        def step(t, _):
-            d = lax.rem(me + t, devices)
+        def start(r, q):
+            d = r * cols + q
             pltpu.make_async_remote_copy(
                 src_ref=send.at[u, d], dst_ref=recv.at[u, me],
                 send_sem=send_sem.at[u], recv_sem=recv_sem.at[u],
-                device_id=place(d), device_id_type=MESH,
+                device_id=(r, q), device_id_type=MESH,
             ).start()
-            return 0
 
         own = pltpu.make_async_copy(send.at[u, me], recv.at[u, me], own_sem.at[u])
         own.start()
-        lax.fori_loop(1, devices, step, 0)
+        everyone(start)
         own.wait()
         some = pl.ds(0, devices - 1)
         pltpu.make_async_copy(recv.at[u, some], recv.at[u, some], recv_sem.at[u]).wait()
@@ -110,7 +169,7 @@
                     matrix[pl.ds(top + TILE, TILE), m * LANES : (m + 1) * LANES] = lower
             return 0
 
-        lax.fori_loop(0, rows, step, 0)
+        lax.fori_loop(0, rows, step, 0, unroll=4)
 
     def product(u):
         if u == 0:
@@ -119,10 +178,8 @@
             dims = (((1,), (0,)), ((), ()))
             left_m[...] = left_m[...].astype(jnp.float32).T.astype(jnp.bfloat16)
         group = 4
-        first = lax.axis_index("row") // group
-
-        def step(b, _):
-            block = lax.rem(first + b, rows // group)
+
+        def step(block, _):
             height = group * 2 * TILE
             left = left_m[pl.ds(pl.multiple_of(block * height, height), height), :]
             sums = lax.dot_general(left, right_m[...], dims, preferred_element_type=jnp.float32)
@@ -138,23 +195,18 @@
                     ssend[u, d] = a
                     ssend[u, d + 1] = b_
 
-            def out_step(t, _):
-                d = block * group * cols + lax.rem(t + me, group * cols)
-
-                @pl.when(d != me)
-                def _():
-                    pltpu.make_async_remote_copy(
-                        src_ref=ssend.at[u, d], dst_ref=srecv.at[u, me],
-                        send_sem=ssend_sem.at[u], recv_sem=srecv_sem.at[u],
-                        device_id=place(d), device_id_type=MESH,
-                    ).start()
-
-                return 0
-
-            lax.fori_loop(0, group * cols, out_step, 0)
             return 0
 
         lax.fori_loop(0, rows // group, step, 0)
+
+        def start(r, q):
+            pltpu.make_async_remote_copy(
+                src_ref=ssend.at[u, r * cols + q], dst_ref=srecv.at[u, me],
+                send_sem=ssend_sem.at[u], recv_sem=srecv_sem.at[u],
+                device_id=(r, q), device_id_type=MESH,
+            ).start()
+
+        everyone(start)
         own = pltpu.make_async_copy(ssend.at[u, me], srecv.at[u, me], sown_sem.at[u])
         own.start()
         own.wait()
@@ -172,42 +224,53 @@
         lax.fori_loop(0, C // group, step, 0)
 
     def finish(u, s):
-        sums = left_f[pl.ds(s, C, stride=TILE), :]
-        normed = norm(sums, gain_t[u, 1], shift_t[u, 1]).astype(jnp.bfloat16)
+        sums = jnp.concatenate(
+            [left_f[pl.ds(s + k, C, stride=TILE), :] for k in range(WIDE)], axis=1
+        )
+        normed = norm(sums, wide(gain_t[u, 1]), wide(shift_t[u, 1])).astype(jnp.bfloat16)
         branch = jnp.dot(w_out_t[u], normed, preferred_element_type=jnp.float32)
-        return (pair_t[s] + gate_t[s] * branch).astype(jnp.bfloat16).astype(jnp.float32)
-
-    def first_step(s, _):
-        values = jnp.concatenate([pair[s], pair[s + TILE]], axis=0)
-        project(0, s, values.astype(jnp.float32).T)
+        return (pair_t[s // WIDE] + gate_t[s // WIDE] * branch).astype(jnp.bfloat16)
+
+    def first_step(n, _):
+        s = n * WIDE
+        blocks = [
+            jnp.concatenate([pair[s + k], pair[s + k + TILE]], axis=0).T for k in range(WIDE)
+        ]
+        project(0, s, jnp.concatenate(blocks, axis=1).astype(jnp.float32))
         return 0
 
-    lax.fori_loop(0, TILE, first_step, 0)
+    loads[5].wait()
+    lax.fori_loop(0, TILE // WIDE, first_step, 0)
+    pl.semaphore_wait(barrier, rows + cols - 2)
+    greet_col(ready)
     pack(0)
-    pl.semaphore_wait(barrier, devices - 1)
+    pl.semaphore_wait(ready, cols - 1)
     exchange(0)
     gather(0)
     product(0)
     widen(0)
 
-    def second_step(s, _):
-        project(1, s, finish(0, s))
+    def second_step(n, _):
+        project(1, n * WIDE, finish(0, n * WIDE).astype(jnp.float32))
         return 0
 
-    lax.fori_loop(0, TILE, second_step, 0)
+    lax.fori_loop(0, TILE // WIDE, second_step, 0)
     pack(1)
     exchange(1)
     gather(1)
     product(1)
     widen(1)
 
-    def last_step(s, _):
-        values = finish(1, s).T.astype(jnp.bfloat16)
-        out[s] = values[:HALF]
-        out[s + TILE] = values[HALF:]
+    def last_step(n, _):
+        s = n * WIDE
+        values = finish(1, s)
+        for k in range(WIDE):
+            block = values[:, k * LANES : (k + 1) * LANES].T
+            out[s + k] = block[:HALF]
+            out[s + k + TILE] = block[HALF:]
         return 0
 
-    lax.fori_loop(0, TILE, last_step, 0)
+    lax.fori_loop(0, TILE // WIDE, last_step, 0)
     some = pl.ds(0, devices - 1)
     for u in range(2):
         pltpu.make_async_copy(send.at[u, some], send.at[u, some], send_sem.at[u]).wait()
@@ -224,15 +287,21 @@
         return pl.pallas_call(
             functools.partial(kernel, rows, cols),
             out_shape=jax.ShapeDtypeStruct(pair_rep.shape, bf16),
-            in_specs=[vmem] * 6,
+            in_specs=[pl.BlockSpec(memory_space=pl.ANY)] * 6,
             out_specs=vmem,
             scratch_shapes=[
+                pltpu.VMEM(pair_rep.shape, bf16),
+                pltpu.VMEM(w_proj.shape, bf16),
+                pltpu.VMEM(w_gate.shape, bf16),
+                pltpu.VMEM(w_out.shape, bf16),
+                pltpu.VMEM(norm_gain.shape, f32),
+                pltpu.VMEM(norm_shift.shape, f32),
                 pltpu.VMEM((2, 5 * C, C), bf16),
                 pltpu.VMEM((2, C, C), bf16),
                 pltpu.VMEM((2, 2, C, LANES), f32),
                 pltpu.VMEM((2, 2, C, LANES), f32),
-                pltpu.VMEM((TILE, C, LANES), f32),
-                pltpu.VMEM((TILE, C, LANES), f32),
+                pltpu.VMEM((TILE // WIDE, C, WIDE * LANES), f32),
+                pltpu.VMEM((TILE // WIDE, C, WIDE * LANES), f32),
                 pltpu.VMEM((C * TILE, LANES), f32),
                 pltpu.VMEM((C * TILE, LANES), f32),
                 pltpu.VMEM((2, devices, 2, TILE, LANES), bf16),
@@ -242,7 +311,8 @@
                 pltpu.VMEM((RES, RES), bf16),
                 pltpu.VMEM((RES, RES), bf16),
             ]
-            + [pltpu.SemaphoreType.DMA((2,))] * 6,
+            + [pltpu.SemaphoreType.DMA((2,))] * 6
+            + [pltpu.SemaphoreType.DMA((6,)), pltpu.SemaphoreType.REGULAR],
             compiler_params=pltpu.CompilerParams(
                 collective_id=0, has_side_effects=True, vmem_limit_bytes=48 << 20
             ),

time: 94.2 us -> 75.3 us (0.80)
  Pallas kernels: 88 us -> 69.1 us
    pallas_call x1, Pallas kernels: 88 us -> 69.1 us  [body(): pl.pallas_call(functools.partial(kernel, rows, cols), out_shape=jax.Shape...]
where the time goes in v2:
time: 75.3 us; the launch traced here: 75 us
  Pallas kernels  69.1 us (92%)
  local copies, waits for them, and re-layouts  5.83 us (8%)
    pallas_call x1, Pallas kernels, body(): pl.pallas_call(functools.partial(kernel, rows, cols), out_shape=jax.Shape...  69.1 us
    unnamed x13, local copies, waits for them, and re-layouts  5.83 us

profile of v2, /device:TPU:1, one launch (start us, length us, event | category | flops | bytes accessed | tf_op | source)
XLA Modules:
  0.0 75.0 jit_solution(9058846321241539886)
XLA Ops:
  0.0 0.0 copy-start
  0.0 1.0 %copy-done = bf16[32,64,128]{2,1,0:T(8,128)(2,1)S(1)} copy-done((bf16[32,64,128]{2,1,0:T(8,128)(2,1)S(1)}, bf16[32,64,128]{2,1,0:T(8,128)(2,1)}, u32[]{:S(2)}) %copy-start) | copy-done | bytes 524312
  1.0 0.0 copy-start.1
  1.0 0.9 %copy-done.1 = bf16[2,128,512]{2,1,0:T(8,128)(2,1)S(1)} copy-done((bf16[2,128,512]{2,1,0:T(8,128)(2,1)S(1)}, bf16[2,128,512]{2,1,0:T(8,128)(2,1)}, u32[]{:S(2)}) %copy-start.1) | copy-done | bytes 262168
  2.0 0.0 copy-start.2
  2.0 0.8 %copy-done.2 = bf16[2,128,128]{2,1,0:T(8,128)(2,1)S(1)} copy-done((bf16[2,128,128]{2,1,0:T(8,128)(2,1)S(1)}, bf16[2,128,128]{2,1,0:T(8,128)(2,1)}, u32[]{:S(2)}) %copy-start.2) | copy-done | bytes 65560
  2.8 0.0 copy-start.3
  2.8 0.8 %copy-done.3 = bf16[2,128,128]{2,1,0:T(8,128)(2,1)S(1)} copy-done((bf16[2,128,128]{2,1,0:T(8,128)(2,1)S(1)}, bf16[2,128,128]{2,1,0:T(8,128)(2,1)}, u32[]{:S(2)}) %copy-start.3) | copy-done | bytes 65560
  3.7 0.0 copy-start.4
  3.7 0.7 copy-done.4
  4.4 0.0 copy-start.5
  4.4 0.7 copy-done.5
  5.0 69.1 %shard_map.64 = bf16[32,64,128]{2,1,0:T(8,128)(2,1)S(1)} custom-call(bf16[32,64,128]{2,1,0:T(8,128)(2,1)S(1)} %copy-done, bf16[2,128,512]{2,1,0:T(8,128)(2,1)S(1)} %copy-done.1, bf16[2,128,128]{2,1,0:T(8,128)(2,1)S(1)} %copy-done.2, bf16[2,128,128]{2,1,0:T(8,128)(2,1)S(1)} %copy-done.3, f32[2,2,128]{2,1,0:T(2,128)S(1)} %copy-done.4, f32[2,2,128]{2,1,0:T(2,128)S(1)} %copy-done.5), custom_call_target="tpu_custom_call" | custom-call | tf_op jit(solution)/shard_map/pallas_call | solution.py:287
  74.2 0.8 %copy.8 = bf16[32,64,128]{2,1,0:T(8,128)(2,1)} copy(bf16[32,64,128]{2,1,0:T(8,128)(2,1)S(1)} %shard_map.64) | data formatting | bytes 1048576
Async XLA Ops:
  0.0 1.0 %copy-start = (bf16[32,64,128]{2,1,0:T(8,128)(2,1)S(1)}, bf16[32,64,128]{2,1,0:T(8,128)(2,1)}, u32[]{:S(2)}) copy-start(bf16[32,64,128]{2,1,0:T(8,128)(2,1)} %pair_h.1) | copy-start | bytes 1572868
  1.0 0.9 %copy-start.1 = (bf16[2,128,512]{2,1,0:T(8,128)(2,1)S(1)}, bf16[2,128,512]{2,1,0:T(8,128)(2,1)}, u32[]{:S(2)}) copy-start(bf16[2,128,512]{2,1,0:T(8,128)(2,1)} %w_proj_h.1) | copy-start | bytes 786436
  2.0 0.8 %copy-start.2 = (bf16[2,128,128]{2,1,0:T(8,128)(2,1)S(1)}, bf16[2,128,128]{2,1,0:T(8,128)(2,1)}, u32[]{:S(2)}) copy-start(bf16[2,128,128]{2,1,0:T(8,128)(2,1)} %w_gate_h.1) | copy-start | bytes 196612
  2.8 0.8 %copy-start.3 = (bf16[2,128,128]{2,1,0:T(8,128)(2,1)S(1)}, bf16[2,128,128]{2,1,0:T(8,128)(2,1)}, u32[]{:S(2)}) copy-start(bf16[2,128,128]{2,1,0:T(8,128)(2,1)} %w_out_h.1) | copy-start | bytes 196612
  3.7 0.7 copy-start.4
  4.4 0.7 copy-start.5

commit v3 on v2

v3 whole, which is shorter than its diff:
```python
import functools

import jax
import jax.numpy as jnp
from jax import lax
from jax.experimental import pallas as pl
from jax.experimental.pallas import tpu as pltpu
from jax.sharding import PartitionSpec as P

MESH = pl.DeviceIdType.MESH
EPSILON = 1e-05
C = 128
RES = 512
LANES = 128
TILE = 16
WIDE = 4
STEPS = TILE // WIDE
HALF = 64
HIGH = 32
BF16, F32 = jnp.bfloat16, jnp.float32


def sigmoid(x):
    return 0.5 * jnp.tanh(0.5 * x) + 0.5


def norm(values, gain, shift):
    average = jnp.sum(values, axis=0, keepdims=True) * (1.0 / C)
    centred = values - average
    variance = jnp.sum(centred * centred, axis=0, keepdims=True) * (1.0 / C)
    return centred * lax.rsqrt(variance + EPSILON) * gain + shift


def swap(first, second):
    return (
        jnp.concatenate([first[:, :HALF], second[:, :HALF]], axis=1),
        jnp.concatenate([first[:, HALF:], second[:, HALF:]], axis=1),
    )


def far_first():
    def hops(offset):
        return sum(min(v, 4 - v) for v in (offset // 16, offset // 4 % 4, offset % 4))

    return sorted(range(64), key=lambda offset: -hops(offset))


def kernel(
    rows, cols, pair_h, w_proj_h, w_gate_h, w_out_h, gain_h, shift_h, out,
    pair, w_proj, w_gate, w_out, gain, shift,
    w_in_t, w_out_t, gain_t, shift_t, pair_t, gate_t, normed_t, left_f, right_f,
    send, recv, ssend, srecv, left_m, right_m, left_t, partial,
    send_sem, recv_sem, own_sem, ssend_sem, srecv_sem, sown_sem, in_sem, ready,
):
    devices = rows * cols
    row, col = lax.axis_index("row"), lax.axis_index("col")
    me = row * cols + col
    x, y, z, core = row // 4, lax.rem(col, 4), lax.rem(row // 2, 2) * 2 + col // 4, lax.rem(row, 2)
    parity = (1 - core, core)

    loads = [
        pltpu.make_async_copy(source, target, in_sem.at[k])
        for k, (source, target) in enumerate((
            (w_proj_h, w_proj), (w_gate_h, w_gate), (w_out_h, w_out),
            (gain_h, gain), (shift_h, shift), (pair_h, pair),
        ))
    ]
    for load in loads:
        load.start()

    barrier = pltpu.get_barrier_semaphore()

    def greet_row(t, _):
        pl.semaphore_signal(
            barrier, inc=1, device_id=(lax.rem(row + t, rows), col), device_id_type=MESH
        )
        return 0

    def greet_col(semaphore):
        def step(t, _):
            pl.semaphore_signal(
                semaphore, inc=1, device_id=(row, lax.rem(col + t, cols)), device_id_type=MESH
            )
            return 0

        lax.fori_loop(1, cols, step, 0)

    lax.fori_loop(1, rows, greet_row, 0)
    greet_col(barrier)

    def everyone(group, start):
        offsets = far_first()[: 64 - group]
        for k in range(0, len(offsets), 5):
            part = offsets[k : k + 5]
            digits = sum(offset * 64**n for n, offset in enumerate(part))

            def step(_, rest):
                offset = lax.rem(rest, 64)
                x_ = lax.rem(x + offset // 16, 4)
                y_ = lax.rem(y + lax.rem(offset // 4, 4), 4)
                z_ = lax.rem(z + lax.rem(offset, 4), 4)
                start(x_ * 4 + (z_ // 2) * 2 + parity[group], lax.rem(z_, 2) * 4 + y_)
                return rest // 64

            lax.fori_loop(0, len(part), step, jnp.int32(digits))

    def turn_in(u):
        w_in_t[u, : 4 * C, :] = w_proj[u].astype(F32).T.astype(BF16)
        w_in_t[u, 4 * C :, :] = w_gate[u].astype(F32).T.astype(BF16)
        gain_t[u, 0] = jnp.broadcast_to(gain[u, 0:1, :], (C, LANES)).T
        shift_t[u, 0] = jnp.broadcast_to(shift[u, 0:1, :], (C, LANES)).T

    def turn_out(u):
        w_out_t[u] = w_out[u].astype(F32).T.astype(BF16)
        gain_t[u, 1] = jnp.broadcast_to(gain[u, 1:2, :], (C, LANES)).T
        shift_t[u, 1] = jnp.broadcast_to(shift[u, 1:2, :], (C, LANES)).T

    def wide(block):
        return jnp.concatenate([block] * WIDE, axis=1)

    def project(u, n, values):
        normed = norm(values.astype(F32), wide(gain_t[u, 0]), wide(shift_t[u, 0])).astype(BF16)
        mixed = jnp.dot(w_in_t[u, : 4 * C], normed, preferred_element_type=F32)
        left = sigmoid(mixed[:C]) * mixed[C : 2 * C]
        right = sigmoid(mixed[2 * C : 3 * C]) * mixed[3 * C :]
        for k in range(WIDE):
            lanes = slice(k * LANES, (k + 1) * LANES)
            left_f[pl.ds(n * WIDE + k, C, stride=TILE), :] = left[:, lanes]
            right_f[pl.ds(n * WIDE + k, C, stride=TILE), :] = right[:, lanes]
        normed_t[n] = normed
        pair_t[n] = values

    def gates(u):
        def step(n, _):
            mixed = jnp.dot(w_in_t[u, 4 * C :], normed_t[n], preferred_element_type=F32)
            gate_t[n] = sigmoid(mixed)
            return 0

        lax.fori_loop(0, STEPS, step, 0)

    def pack(u):
        size = 8

        def step(g, _):
            for side, source in ((0, left_f), (1, right_f)):
                block = source[pl.ds(pl.multiple_of(g * size * TILE, size * TILE), size * TILE), :]
                send[u, pl.ds(g * size, size), side] = block.reshape(size, TILE, LANES).astype(BF16)
            return 0

        lax.fori_loop(0, C // size, step, 0)

    def exchange(u):
        for group in range(2):

            def start(r, q, group=group):
                d = r * cols + q
                pltpu.make_async_remote_copy(
                    src_ref=send.at[u, d], dst_ref=recv.at[u, me],
                    send_sem=send_sem.at[u], recv_sem=recv_sem.at[u, group],
                    device_id=(r, q), device_id_type=MESH,
                ).start()

            everyone(group, start)
        own = pltpu.make_async_copy(send.at[u, me], recv.at[u, me], own_sem.at[u])
        own.start()
        own.wait()

    def arrived(u, group):
        some = pl.ds(0, devices // 2 - group)
        pltpu.make_async_copy(recv.at[u, some], recv.at[u, some], recv_sem.at[u, group]).wait()

    def gather(u, group):
        def step(n, _):
            r = 2 * n + parity[group]
            for m in range(cols // 2):
                lanes = slice(m * LANES, (m + 1) * LANES)
                for side, matrix in ((0, left_m), (1, right_m)):
                    slot = r if (u, side) == (0, 1) else group * (rows // 2) + n
                    upper, lower = swap(recv[u, r * cols + 2 * m, side], recv[u, r * cols + 2 * m + 1, side])
                    matrix[slot, :TILE, lanes] = upper
                    matrix[slot, TILE:, lanes] = lower
            return 0

        lax.fori_loop(0, rows // 2, step, 0, unroll=4)

    def deliver(u, group, sums):
        sums = sums.astype(BF16)
        for n in range(rows // 2):
            for m in range(cols // 2):
                lanes = slice(m * LANES, (m + 1) * LANES)
                top = n * HIGH
                first, second = swap(
                    sums[top : top + TILE, lanes], sums[top + TILE : top + HIGH, lanes]
                )
                d = (2 * n + parity[group]) * cols + 2 * m
                ssend[u, d] = first
                ssend[u, d + 1] = second

        def start(r, q):
            pltpu.make_async_remote_copy(
                src_ref=ssend.at[u, r * cols + q], dst_ref=srecv.at[u, me],
                send_sem=ssend_sem.at[u], recv_sem=srecv_sem.at[u],
                device_id=(r, q), device_id_type=MESH,
            ).start()

        everyone(group, start)

    def collect(u):
        own = pltpu.make_async_copy(ssend.at[u, me], srecv.at[u, me], sown_sem.at[u])
        own.start()
        own.wait()
        some = pl.ds(0, devices - 1)
        pltpu.make_async_copy(srecv.at[u, some], srecv.at[u, some], srecv_sem.at[u]).wait()
        size = 8

        def step(g, _):
            block = srecv[u, pl.ds(g * size, size)].astype(F32).reshape(size * TILE, LANES)
            left_f[pl.ds(pl.multiple_of(g * size * TILE, size * TILE), size * TILE), :] = block
            return 0

        lax.fori_loop(0, C // size, step, 0)

    def finish(u, n):
        sums = jnp.concatenate(
            [left_f[pl.ds(n * WIDE + k, C, stride=TILE), :] for k in range(WIDE)], axis=1
        )
        normed = norm(sums, wide(gain_t[u, 1]), wide(shift_t[u, 1])).astype(BF16)
        branch = jnp.dot(w_out_t[u], normed, preferred_element_type=F32)
        return (pair_t[n].astype(F32) + gate_t[n] * branch).astype(BF16)

    half = (rows // 2 * HIGH, RES)
    groups = [slice(g * (rows // 2), (g + 1) * (rows // 2)) for g in range(2)]

    for load in loads[:5]:
        load.wait()
    turn_in(0)
    loads[5].wait()

    def first_step(n, _):
        s = n * WIDE
        blocks = [
            jnp.concatenate([pair[s + k], pair[s + k + TILE]], axis=0).T for k in range(WIDE)
        ]
        project(0, n, jnp.concatenate(blocks, axis=1))
        return 0

    lax.fori_loop(0, STEPS // 2, first_step, 0)
    pl.semaphore_wait(barrier, rows + cols - 2)
    greet_col(ready)
    lax.fori_loop(STEPS // 2, STEPS, first_step, 0)
    pack(0)
    pl.semaphore_wait(ready, cols - 1)
    exchange(0)
    gates(0)
    turn_out(0)
    turn_in(1)
    turn_out(1)
    arrived(0, 0)
    gather(0, 0)
    arrived(0, 1)
    gather(0, 1)
    for group in range(2):
        sums = lax.dot_general(
            left_m[groups[group]].reshape(half), right_m[...].reshape(RES, RES),
            (((1,), (1,)), ((), ())), preferred_element_type=F32,
        )
        deliver(0, group, sums)
    collect(0)

    def second_step(n, _):
        project(1, n, finish(0, n))
        return 0

    lax.fori_loop(0, STEPS, second_step, 0)
    pack(1)
    exchange(1)
    gates(1)
    depth = rows // 2 * HIGH
    for group in range(2):
        arrived(1, group)
        gather(1, group)
        turned = left_m[groups[group]].reshape(half).astype(F32).T.astype(BF16)
        if group == 1:
            left_t[...] = turned.reshape(rows // 2, 2, HIGH, depth)
        else:
            partial[...] = jnp.dot(
                turned, right_m[groups[0]].reshape(half), preferred_element_type=F32
            ).reshape(rows // 2, 2, HIGH, RES)
    for group in range(2):
        left = left_t[:, parity[group]].reshape(depth, depth)
        sums = jnp.dot(left, right_m[groups[1]].reshape(half), preferred_element_type=F32)
        deliver(1, group, partial[:, parity[group]].reshape(half) + sums)
    collect(1)

    def last_step(n, _):
        s = n * WIDE
        values = finish(1, n)
        for k in range(WIDE):
            block = values[:, k * LANES : (k + 1) * LANES].T
            out[s + k] = block[:HALF]
            out[s + k + TILE] = block[HALF:]
        return 0

    lax.fori_loop(0, STEPS, last_step, 0)
    some = pl.ds(0, devices - 1)
    for u in range(2):
        pltpu.make_async_copy(send.at[u, some], send.at[u, some], send_sem.at[u]).wait()
        pltpu.make_async_copy(ssend.at[u, some], ssend.at[u, some], ssend_sem.at[u]).wait()


def solution(mesh):
    rows, cols = mesh.shape["row"], mesh.shape["col"]
    devices = rows * cols
    vmem = pl.BlockSpec(memory_space=pltpu.VMEM)
    dma = pltpu.SemaphoreType.DMA

    def body(pair_rep, w_proj, w_gate, w_out, norm_gain, norm_shift):
        arguments = (pair_rep, w_proj, w_gate, w_out, norm_gain, norm_shift)
        return pl.pallas_call(
            functools.partial(kernel, rows, cols),
            out_shape=jax.ShapeDtypeStruct(pair_rep.shape, BF16),
            in_specs=[pl.BlockSpec(memory_space=pl.ANY)] * 6,
            out_specs=vmem,
            scratch_shapes=[pltpu.VMEM(a.shape, a.dtype) for a in arguments]
            + [
                pltpu.VMEM((2, 5 * C, C), BF16),
                pltpu.VMEM((2, C, C), BF16),
                pltpu.VMEM((2, 2, C, LANES), F32),
                pltpu.VMEM((2, 2, C, LANES), F32),
                pltpu.VMEM((STEPS, C, WIDE * LANES), BF16),
                pltpu.VMEM((STEPS, C, WIDE * LANES), F32),
                pltpu.VMEM((STEPS, C, WIDE * LANES), BF16),
                pltpu.VMEM((C * TILE, LANES), F32),
                pltpu.VMEM((C * TILE, LANES), F32),
                pltpu.VMEM((2, devices, 2, TILE, LANES), BF16),
                pltpu.VMEM((2, devices, 2, TILE, LANES), BF16),
                pltpu.VMEM((2, devices, TILE, LANES), BF16),
                pltpu.VMEM((2, devices, TILE, LANES), BF16),
                pltpu.VMEM((rows, HIGH, RES), BF16),
                pltpu.VMEM((rows, HIGH, RES), BF16),
                pltpu.VMEM((rows // 2, 2, HIGH, RES // 2), BF16),
                pltpu.VMEM((rows // 2, 2, HIGH, RES), F32),
            ]
            + [dma((2,)), dma((2, 2)), dma((2,)), dma((2,)), dma((2,)), dma((2,)), dma((6,))]
            + [pltpu.SemaphoreType.REGULAR],
            compiler_params=pltpu.CompilerParams(
                collective_id=0, has_side_effects=True, vmem_limit_bytes=63 << 20
            ),
        )(*arguments)

    in_specs = (P("row", "col", None), P(), P(), P(), P(), P())
    return jax.shard_map(
        body, mesh=mesh, in_specs=in_specs, out_specs=P("row", "col", None), check_vma=False
    )
```

time: 75.3 us -> 69.1 us (0.918)
  local copies, waits for them, and re-layouts: 5.83 us -> 1.87 us
  Pallas kernels: 69.1 us -> 67.1 us
    unnamed x13 -> x1, local copies, waits for them, and re-layouts: 5.83 us -> 1.87 us
    pallas_call x1, Pallas kernels: 69.1 us -> 67.1 us  [body(): pl.pallas_call(functools.partial(kernel, rows, cols), out_shape=jax.Shape...]
where the time goes in v3:
time: 69.1 us; the launch traced here: 68.9 us
  Pallas kernels  67.1 us (97%)
  local copies, waits for them, and re-layouts  1.87 us (3%)
    pallas_call x1, Pallas kernels, body(): pl.pallas_call(functools.partial(kernel, rows, cols), out_shape=jax.Shape...  67.1 us
    unnamed x1, local copies, waits for them, and re-layouts  1.87 us

profile of v3, /device:TPU:1, one launch (start us, length us, event | category | flops | bytes accessed | tf_op | source)
XLA Modules:
  0.0 68.9 jit_solution(3012858694230475971)
XLA Ops:
  0.0 67.1 %shard_map.64 = bf16[32,64,128]{2,1,0:T(8,128)(2,1)} custom-call(bf16[32,64,128]{2,1,0:T(8,128)(2,1)} %pair_h.1, bf16[2,128,512]{2,1,0:T(8,128)(2,1)} %w_proj_h.1, bf16[2,128,128]{2,1,0:T(8,128)(2,1)} %w_gate_h.1, bf16[2,128,128]{2,1,0:T(8,128)(2,1)} %w_out_h.1, f32[2,2,128]{2,1,0:T(2,128)} %gain_h.1, f32[2,2,128]{2,1,0:T(2,128)} %shift_h.1), custom_call_target="tpu_custom_call" | custom-call | tf_op jit(solution)/shard_map/pallas_call | solution.py:319
  67.1 1.9 %copy.8 = bf16[32,64,128]{2,1,0:T(8,128)(2,1)} copy(bf16[32,64,128]{2,1,0:T(8,128)(2,1)} %shard_map.64) | data formatting | bytes 1048576

commit v4 on v3

--- a/solution.py
+++ b/solution.py
@@ -13,7 +13,7 @@
 RES = 512
 LANES = 128
 TILE = 16
-WIDE = 4
+WIDE = 8
 STEPS = TILE // WIDE
 HALF = 64
 HIGH = 32
@@ -344,9 +344,9 @@
             + [dma((2,)), dma((2, 2)), dma((2,)), dma((2,)), dma((2,)), dma((2,)), dma((6,))]
             + [pltpu.SemaphoreType.REGULAR],
             compiler_params=pltpu.CompilerParams(
-                collective_id=0, has_side_effects=True, vmem_limit_bytes=63 << 20
+                collective_id=0, has_side_effects=True, vmem_limit_bytes=44 << 20
             ),
-        )(*arguments)
+        )(*(pltpu.with_memory_space_constraint(a, pltpu.HBM) for a in arguments))
 
     in_specs = (P("row", "col", None), P(), P(), P(), P(), P())
     return jax.shard_map(

time: 69.1 us -> 65.9 us (0.954)
  Pallas kernels: 67.1 us -> 65 us
  local copies, waits for them, and re-layouts: 1.87 us -> 0.8 us
    pallas_call x1, Pallas kernels: 67.1 us -> 65 us  [body(): pl.pallas_call(functools.partial(kernel, rows, cols), out_shape=jax.Shape...]
    unnamed x1, local copies, waits for them, and re-layouts: 1.87 us -> 0.8 us
where the time goes in v4:
time: 65.9 us; the launch traced here: 65.8 us
  Pallas kernels  65 us (99%)
  local copies, waits for them, and re-layouts  0.8 us (1%)
    pallas_call x1, Pallas kernels, body(): pl.pallas_call(functools.partial(kernel, rows, cols), out_shape=jax.Shape...  65 us

profile of v4, /device:TPU:1, one launch (start us, length us, event | category | flops | bytes accessed | tf_op | source)
XLA Modules:
  0.0 65.8 jit_solution(13293009866218084789)
XLA Ops:
  0.0 65.0 %shard_map.64 = bf16[32,64,128]{2,1,0:T(8,128)(2,1)S(1)} custom-call(bf16[32,64,128]{2,1,0:T(8,128)(2,1)} %pair_h.1, bf16[2,128,512]{2,1,0:T(8,128)(2,1)} %w_proj_h.1, bf16[2,128,128]{2,1,0:T(8,128)(2,1)} %w_gate_h.1, bf16[2,128,128]{2,1,0:T(8,128)(2,1)} %w_out_h.1, f32[2,2,128]{2,1,0:T(2,128)} %gain_h.1, f32[2,2,128]{2,1,0:T(2,128)} %shift_h.1), custom_call_target="tpu_custom_call" | custom-call | tf_op jit(solution)/shard_map/pallas_call | solution.py:319
  65.0 0.8 %copy.8 = bf16[32,64,128]{2,1,0:T(8,128)(2,1)} copy(bf16[32,64,128]{2,1,0:T(8,128)(2,1)S(1)} %shard_map.64) | data formatting | bytes 1048576

commit v5 on v4

v5 whole, which is shorter than its diff:
```python
import functools

import jax
import jax.numpy as jnp
from jax import lax
from jax.experimental import pallas as pl
from jax.experimental.pallas import tpu as pltpu
from jax.sharding import PartitionSpec as P

MESH = pl.DeviceIdType.MESH
EPSILON = 1e-05
C = 128
RES = 512
LANES = 128
TILE = 16
WIDE = 8
STEPS = TILE // WIDE
HALF = 64
HIGH = 32
BF16, F32 = jnp.bfloat16, jnp.float32


def sigmoid(x):
    return 0.5 * jnp.tanh(0.5 * x) + 0.5


def norm(values, gain, shift):
    average = jnp.sum(values, axis=0, keepdims=True) * (1.0 / C)
    centred = values - average
    variance = jnp.sum(centred * centred, axis=0, keepdims=True) * (1.0 / C)
    return centred * lax.rsqrt(variance + EPSILON) * gain + shift


def swap(first, second):
    return (
        jnp.concatenate([first[:, :HALF], second[:, :HALF]], axis=1),
        jnp.concatenate([first[:, HALF:], second[:, HALF:]], axis=1),
    )


def far_first(u, group):
    def steps(offset):
        return offset // 32, offset // 8 % 4, offset // 2 % 4, offset % 2

    def hops(offset):
        return sum(min(v, 4 - v) for v in steps(offset)[:3])

    members = [o for o in range(1, 128) if (steps(o)[3] if u == 0 else steps(o)[2] % 2) == 1 - group]
    return sorted(members, key=lambda o: (-steps(o)[3], -hops(o)))


def kernel(
    rows, cols, pair_h, w_proj_h, w_gate_h, w_out_h, gain_h, shift_h, out,
    pair, w_proj, w_gate, w_out, gain, shift,
    w_in_t, w_out_t, gain_t, shift_t, pair_t, gate_t, normed_t, left_f, right_f,
    send, recv, ssend, srecv, shared_m, shared_t, split_out, split_in,
    send_sem, recv_sem, own_sem, ssend_sem, srecv_sem, sown_sem, in_sem, ready,
):
    devices = rows * cols
    row, col = lax.axis_index("row"), lax.axis_index("col")
    me = row * cols + col
    x, y, z, core = row // 4, lax.rem(col, 4), lax.rem(row // 2, 2) * 2 + col // 4, lax.rem(row, 2)
    parity = (1 - core, core)
    z_lo = (1 - col // 4, col // 4)

    loads = [
        pltpu.make_async_copy(source, target, in_sem.at[k])
        for k, (source, target) in enumerate((
            (w_proj_h, w_proj), (w_gate_h, w_gate), (w_out_h, w_out),
            (gain_h, gain), (shift_h, shift), (pair_h, pair),
        ))
    ]
    for load in loads:
        load.start()

    barrier = pltpu.get_barrier_semaphore()

    def greet_row(t, _):
        pl.semaphore_signal(
            barrier, inc=1, device_id=(lax.rem(row + t, rows), col), device_id_type=MESH
        )
        return 0

    def greet_col(semaphore):
        def step(t, _):
            pl.semaphore_signal(
                semaphore, inc=1, device_id=(row, lax.rem(col + t, cols)), device_id_type=MESH
            )
            return 0

        lax.fori_loop(1, cols, step, 0)

    lax.fori_loop(1, rows, greet_row, 0)
    greet_col(barrier)

    def everyone(u, group, start):
        offsets = far_first(u, group)
        for k in range(0, len(offsets), 4):
            part = offsets[k : k + 4]
            digits = sum(offset * 128**n for n, offset in enumerate(part))

            def step(_, rest):
                x_ = (x + ((rest >> 5) & 3)) & 3
                y_ = (y + ((rest >> 3) & 3)) & 3
                z_ = (z + ((rest >> 1) & 3)) & 3
                core_ = (core + rest) & 1
                start(x_ * 4 + (z_ >> 1) * 2 + core_, (z_ & 1) * 4 + y_)
                return rest >> 7

            lax.fori_loop(0, len(part), step, jnp.int32(digits))

    def turn_in(u):
        w_in_t[u, : 4 * C, :] = w_proj[u].astype(F32).T.astype(BF16)
        w_in_t[u, 4 * C :, :] = w_gate[u].astype(F32).T.astype(BF16)
        gain_t[u, 0] = jnp.broadcast_to(gain[u, 0:1, :], (C, LANES)).T
        shift_t[u, 0] = jnp.broadcast_to(shift[u, 0:1, :], (C, LANES)).T

    def turn_out(u):
        w_out_t[u] = w_out[u].astype(F32).T.astype(BF16)
        gain_t[u, 1] = jnp.broadcast_to(gain[u, 1:2, :], (C, LANES)).T
        shift_t[u, 1] = jnp.broadcast_to(shift[u, 1:2, :], (C, LANES)).T

    def wide(block):
        return jnp.concatenate([block] * WIDE, axis=1)

    def prepare(u, n, values):
        normed = norm(values.astype(F32), wide(gain_t[u, 0]), wide(shift_t[u, 0])).astype(BF16)
        normed_t[n] = normed
        pair_t[n] = values
        return normed

    def operand(u, side, n, normed):
        weights = w_in_t[u, side * 2 * C : (side + 1) * 2 * C]
        mixed = jnp.dot(weights, normed, preferred_element_type=F32)
        product = sigmoid(mixed[:C]) * mixed[C:]
        for k in range(WIDE):
            target = (left_f, right_f)[side]
            target[pl.ds(n * WIDE + k, C, stride=TILE), :] = product[:, k * LANES : (k + 1) * LANES]

    def gates(u):
        def step(n, _):
            mixed = jnp.dot(w_in_t[u, 4 * C :], normed_t[n], preferred_element_type=F32)
            gate_t[n] = sigmoid(mixed)
            return 0

        lax.fori_loop(0, STEPS, step, 0)

    def pack(u, side):
        size = 8
        source = (left_f, right_f)[side]

        def step(g, _):
            block = source[pl.ds(pl.multiple_of(g * size * TILE, size * TILE), size * TILE), :]
            send[u, side, pl.ds(g * size, size)] = block.reshape(size, TILE, LANES).astype(BF16)
            return 0

        lax.fori_loop(0, C // size, step, 0)

    def ship(u, side):
        for group in range(2):

            def start(r, q, group=group):
                pltpu.make_async_remote_copy(
                    src_ref=send.at[u, side, r * cols + q], dst_ref=recv.at[u, side, me],
                    send_sem=send_sem.at[u, side], recv_sem=recv_sem.at[u, side, group],
                    device_id=(r, q), device_id_type=MESH,
                ).start()

            everyone(u, group, start)
        own = pltpu.make_async_copy(send.at[u, side, me], recv.at[u, side, me], own_sem.at[u, side])
        own.start()
        own.wait()

    def gather(u, side, group, matrix):
        some = pl.ds(0, devices // 2 - group)
        pltpu.make_async_copy(
            recv.at[u, side, some], recv.at[u, side, some], recv_sem.at[u, side, group]
        ).wait()
        whole = matrix is shared_m

        def place(source, slot, lanes):
            upper, lower = swap(recv[u, side, source], recv[u, side, source + 1])
            matrix[slot + (slice(0, TILE), lanes)] = upper
            matrix[slot + (slice(TILE, HIGH), lanes)] = lower

        def step_out(n, _):
            r = 2 * n + parity[group]
            for m in range(cols // 2):
                lanes = slice(m * LANES, (m + 1) * LANES)
                place(r * cols + 2 * m, (r,) if whole else (group, n), lanes)
            return 0

        def step_in(r, _):
            for m in range(cols // 4):
                lanes = slice(m * LANES, (m + 1) * LANES)
                if whole:
                    lanes = pl.ds(pl.multiple_of((z_lo[group] * 2 + m) * LANES, LANES), LANES)
                place(r * cols + z_lo[group] * 4 + 2 * m, (r,) if whole else (group, r), lanes)
            return 0

        if u == 0:
            lax.fori_loop(0, rows // 2, step_out, 0, unroll=4)
        else:
            lax.fori_loop(0, rows, step_in, 0, unroll=8)

    def turn_shared():
        shared_t[...] = shared_m[...].reshape(RES, RES).astype(F32).T.astype(BF16)

    def deliver(u, group, sums):
        sums = sums.astype(BF16)
        for n in range(rows // 2 if u == 0 else rows):
            for m in range(cols // 2 if u == 0 else cols // 4):
                lanes = slice(m * LANES, (m + 1) * LANES)
                top = n * HIGH
                first, second = swap(
                    sums[top : top + TILE, lanes], sums[top + TILE : top + HIGH, lanes]
                )
                if u == 0:
                    d = (2 * n + parity[group]) * cols + 2 * m
                else:
                    d = n * cols + z_lo[group] * 4 + 2 * m
                ssend[u, d] = first
                ssend[u, d + 1] = second

        def start(r, q):
            pltpu.make_async_remote_copy(
                src_ref=ssend.at[u, r * cols + q], dst_ref=srecv.at[u, me],
                send_sem=ssend_sem.at[u], recv_sem=srecv_sem.at[u],
                device_id=(r, q), device_id_type=MESH,
            ).start()

        everyone(u, group, start)

    def collect(u):
        own = pltpu.make_async_copy(ssend.at[u, me], srecv.at[u, me], sown_sem.at[u])
        own.start()
        own.wait()
        some = pl.ds(0, devices - 1)
        pltpu.make_async_copy(srecv.at[u, some], srecv.at[u, some], srecv_sem.at[u]).wait()
        size = 8

        def step(g, _):
            block = srecv[u, pl.ds(g * size, size)].astype(F32).reshape(size * TILE, LANES)
            left_f[pl.ds(pl.multiple_of(g * size * TILE, size * TILE), size * TILE), :] = block
            return 0

        lax.fori_loop(0, C // size, step, 0)

    def finish(u, n):
        sums = jnp.concatenate(
            [left_f[pl.ds(n * WIDE + k, C, stride=TILE), :] for k in range(WIDE)], axis=1
        )
        normed = norm(sums, wide(gain_t[u, 1]), wide(shift_t[u, 1])).astype(BF16)
        branch = jnp.dot(w_out_t[u], normed, preferred_element_type=F32)
        return (pair_t[n].astype(F32) + gate_t[n] * branch).astype(BF16)

    for load in loads[:5]:
        load.wait()
    turn_in(0)
    loads[5].wait()

    def first_step(n, _):
        s = n * WIDE
        blocks = [
            jnp.concatenate([pair[s + k], pair[s + k + TILE]], axis=0).T for k in range(WIDE)
        ]
        operand(0, 1, n, prepare(0, n, jnp.concatenate(blocks, axis=1)))
        return 0

    lax.fori_loop(0, STEPS // 2, first_step, 0)
    pl.semaphore_wait(barrier, rows + cols - 2)
    greet_col(ready)
    lax.fori_loop(STEPS // 2, STEPS, first_step, 0)
    pack(0, 1)
    pl.semaphore_wait(ready, cols - 1)
    ship(0, 1)

    def other_operand(u, side):
        def step(n, _):
            operand(u, side, n, normed_t[n])
            return 0

        lax.fori_loop(0, STEPS, step, 0)
        pack(u, side)
        ship(u, side)

    other_operand(0, 0)
    gates(0)
    turn_out(0)
    turn_in(1)
    turn_out(1)
    for group in range(2):
        gather(0, 1, group, shared_m)
    turn_shared()
    for group in range(2):
        gather(0, 0, group, split_out)
        left = split_out[group].reshape(RES // 2, RES)
        deliver(0, group, jnp.dot(left, shared_t[...], preferred_element_type=F32))
    collect(0)

    def second_step(n, _):
        operand(1, 0, n, prepare(1, n, finish(0, n)))
        return 0

    lax.fori_loop(0, STEPS, second_step, 0)
    pack(1, 0)
    ship(1, 0)
    other_operand(1, 1)
    gates(1)
    for group in range(2):
        gather(1, 0, group, shared_m)
    turn_shared()
    for group in range(2):
        gather(1, 1, group, split_in)
        right = split_in[group].reshape(RES, RES // 2)
        deliver(1, group, jnp.dot(shared_t[...], right, preferred_element_type=F32))
    collect(1)

    def last_step(n, _):
        s = n * WIDE
        values = finish(1, n)
        for k in range(WIDE):
            block = values[:, k * LANES : (k + 1) * LANES].T
            out[s + k] = block[:HALF]
            out[s + k + TILE] = block[HALF:]
        return 0

    lax.fori_loop(0, STEPS, last_step, 0)
    some = pl.ds(0, devices - 1)
    for u in range(2):
        for side in range(2):
            pltpu.make_async_copy(
                send.at[u, side, some], send.at[u, side, some], send_sem.at[u, side]
            ).wait()
        pltpu.make_async_copy(ssend.at[u, some], ssend.at[u, some], ssend_sem.at[u]).wait()


def solution(mesh):
    rows, cols = mesh.shape["row"], mesh.shape["col"]
    devices = rows * cols
    vmem = pl.BlockSpec(memory_space=pltpu.VMEM)
    dma = pltpu.SemaphoreType.DMA

    def body(pair_rep, w_proj, w_gate, w_out, norm_gain, norm_shift):
        arguments = (pair_rep, w_proj, w_gate, w_out, norm_gain, norm_shift)
        return pl.pallas_call(
            functools.partial(kernel, rows, cols),
            out_shape=jax.ShapeDtypeStruct(pair_rep.shape, BF16),
            in_specs=[pl.BlockSpec(memory_space=pl.ANY)] * 6,
            out_specs=vmem,
            scratch_shapes=[pltpu.VMEM(a.shape, a.dtype) for a in arguments]
            + [
                pltpu.VMEM((2, 5 * C, C), BF16),
                pltpu.VMEM((2, C, C), BF16),
                pltpu.VMEM((2, 2, C, LANES), F32),
                pltpu.VMEM((2, 2, C, LANES), F32),
                pltpu.VMEM((STEPS, C, WIDE * LANES), BF16),
                pltpu.VMEM((STEPS, C, WIDE * LANES), F32),
                pltpu.VMEM((STEPS, C, WIDE * LANES), BF16),
                pltpu.VMEM((C * TILE, LANES), F32),
                pltpu.VMEM((C * TILE, LANES), F32),
                pltpu.VMEM((2, 2, devices, TILE, LANES), BF16),
                pltpu.VMEM((2, 2, devices, TILE, LANES), BF16),
                pltpu.VMEM((2, devices, TILE, LANES), BF16),
                pltpu.VMEM((2, devices, TILE, LANES), BF16),
                pltpu.VMEM((rows, HIGH, RES), BF16),
                pltpu.VMEM((RES, RES), BF16),
                pltpu.VMEM((2, rows // 2, HIGH, RES), BF16),
                pltpu.VMEM((2, rows, HIGH, RES // 2), BF16),
            ]
            + [dma((2, 2)), dma((2, 2, 2)), dma((2, 2)), dma((2,)), dma((2,)), dma((2,)), dma((6,))]
            + [pltpu.SemaphoreType.REGULAR],
            compiler_params=pltpu.CompilerParams(
                collective_id=0, has_side_effects=True, vmem_limit_bytes=44 << 20
            ),
        )(*(pltpu.with_memory_space_constraint(a, pltpu.HBM) for a in arguments))

    in_specs = (P("row", "col", None), P(), P(), P(), P(), P())
    return jax.shard_map(
        body, mesh=mesh, in_specs=in_specs, out_specs=P("row", "col", None), check_vma=False
    )
```

time: 65.9 us -> 61.2 us (0.929)
  Pallas kernels: 65 us -> 60.2 us
    pallas_call x1, Pallas kernels: 65 us -> 60.2 us  [body(): pl.pallas_call(functools.partial(kernel, rows, cols), out_shape=jax.Shape...]
where the time goes in v5:
time: 61.2 us; the launch traced here: 61 us
  Pallas kernels  60.2 us (98%)
  local copies, waits for them, and re-layouts  0.8 us (1%)
    pallas_call x1, Pallas kernels, body(): pl.pallas_call(functools.partial(kernel, rows, cols), out_shape=jax.Shape...  60.2 us

profile of v5, /device:TPU:1, one launch (start us, length us, event | category | flops | bytes accessed | tf_op | source)
XLA Modules:
  0.0 61.0 jit_solution(12209615196118188254)
XLA Ops:
  0.0 60.2 %shard_map.64 = bf16[32,64,128]{2,1,0:T(8,128)(2,1)S(1)} custom-call(bf16[32,64,128]{2,1,0:T(8,128)(2,1)} %pair_h.1, bf16[2,128,512]{2,1,0:T(8,128)(2,1)} %w_proj_h.1, bf16[2,128,128]{2,1,0:T(8,128)(2,1)} %w_gate_h.1, bf16[2,128,128]{2,1,0:T(8,128)(2,1)} %w_out_h.1, f32[2,2,128]{2,1,0:T(2,128)} %gain_h.1, f32[2,2,128]{2,1,0:T(2,128)} %shift_h.1), custom_call_target="tpu_custom_call" | custom-call | tf_op jit(solution)/shard_map/pallas_call | solution.py:346
  60.2 0.8 %copy.8 = bf16[32,64,128]{2,1,0:T(8,128)(2,1)} copy(bf16[32,64,128]{2,1,0:T(8,128)(2,1)S(1)} %shard_map.64) | data formatting | bytes 1048576

commit v6 on v5

--- a/solution.py
+++ b/solution.py
@@ -93,21 +93,15 @@
     lax.fori_loop(1, rows, greet_row, 0)
     greet_col(barrier)
 
+    xs = [((x + k) & 3) * 4 for k in range(4)]
+    ys = [(y + k) & 3 for k in range(4)]
+    zs = [((((z + k) & 3) >> 1) * 2, (((z + k) & 3) & 1) * 4) for k in range(4)]
+    cs = [core, 1 - core]
+
     def everyone(u, group, start):
-        offsets = far_first(u, group)
-        for k in range(0, len(offsets), 4):
-            part = offsets[k : k + 4]
-            digits = sum(offset * 128**n for n, offset in enumerate(part))
-
-            def step(_, rest):
-                x_ = (x + ((rest >> 5) & 3)) & 3
-                y_ = (y + ((rest >> 3) & 3)) & 3
-                z_ = (z + ((rest >> 1) & 3)) & 3
-                core_ = (core + rest) & 1
-                start(x_ * 4 + (z_ >> 1) * 2 + core_, (z_ & 1) * 4 + y_)
-                return rest >> 7
-
-            lax.fori_loop(0, len(part), step, jnp.int32(digits))
+        for offset in far_first(u, group):
+            dx, dy, dz, dc = offset // 32, offset // 8 % 4, offset // 2 % 4, offset % 2
+            start(xs[dx] + zs[dz][0] + cs[dc], zs[dz][1] + ys[dy])
 
     def turn_in(u):
         w_in_t[u, : 4 * C, :] = w_proj[u].astype(F32).T.astype(BF16)
@@ -156,8 +150,8 @@
 
         lax.fori_loop(0, C // size, step, 0)
 
-    def ship(u, side):
-        for group in range(2):
+    def ship(u, side, which=(0, 1)):
+        for group in which:
 
             def start(r, q, group=group):
                 pltpu.make_async_remote_copy(
@@ -167,9 +161,12 @@
                 ).start()
 
             everyone(u, group, start)
-        own = pltpu.make_async_copy(send.at[u, side, me], recv.at[u, side, me], own_sem.at[u, side])
-        own.start()
-        own.wait()
+        if 1 in which:
+            own = pltpu.make_async_copy(
+                send.at[u, side, me], recv.at[u, side, me], own_sem.at[u, side]
+            )
+            own.start()
+            own.wait()
 
     def gather(u, side, group, matrix):
         some = pl.ds(0, devices // 2 - group)
@@ -282,7 +279,7 @@
 
         lax.fori_loop(0, STEPS, step, 0)
         pack(u, side)
-        ship(u, side)
+        ship(u, side, (0,))
 
     other_operand(0, 0)
     gates(0)
@@ -291,6 +288,8 @@
     turn_out(1)
     for group in range(2):
         gather(0, 1, group, shared_m)
+        if group == 0:
+            ship(0, 0, (1,))
     turn_shared()
     for group in range(2):
         gather(0, 0, group, split_out)
@@ -309,6 +308,8 @@
     gates(1)
     for group in range(2):
         gather(1, 0, group, shared_m)
+        if group == 0:
+            ship(1, 1, (1,))
     turn_shared()
     for group in range(2):
         gather(1, 1, group, split_in)

time: 61.2 us -> 59.7 us (0.975)
  Pallas kernels: 60.2 us -> 58.8 us
    pallas_call x1, Pallas kernels: 60.2 us -> 58.8 us  [body(): pl.pallas_call(functools.partial(kernel, rows, cols), out_shape=jax.Shape...]
where the time goes in v6:
time: 59.7 us; the launch traced here: 59.6 us
  Pallas kernels  58.8 us (98%)
  local copies, waits for them, and re-layouts  0.8 us (1%)
    pallas_call x1, Pallas kernels, body(): pl.pallas_call(functools.partial(kernel, rows, cols), out_shape=jax.Shape...  58.8 us

profile of v6, /device:TPU:1, one launch (start us, length us, event | category | flops | bytes accessed | tf_op | source)
XLA Modules:
  0.0 59.6 jit_solution(9791404226008022797)
XLA Ops:
  0.0 58.8 %shard_map.64 = bf16[32,64,128]{2,1,0:T(8,128)(2,1)S(1)} custom-call(bf16[32,64,128]{2,1,0:T(8,128)(2,1)} %pair_h.1, bf16[2,128,512]{2,1,0:T(8,128)(2,1)} %w_proj_h.1, bf16[2,128,128]{2,1,0:T(8,128)(2,1)} %w_gate_h.1, bf16[2,128,128]{2,1,0:T(8,128)(2,1)} %w_out_h.1, f32[2,2,128]{2,1,0:T(2,128)} %gain_h.1, f32[2,2,128]{2,1,0:T(2,128)} %shift_h.1), custom_call_target="tpu_custom_call" | custom-call | tf_op jit(solution)/shard_map/pallas_call | solution.py:347
  58.8 0.8 %copy.8 = bf16[32,64,128]{2,1,0:T(8,128)(2,1)} copy(bf16[32,64,128]{2,1,0:T(8,128)(2,1)S(1)} %shard_map.64) | data formatting | bytes 1048576

commit v7 on v6

--- a/solution.py
+++ b/solution.py
@@ -13,15 +13,11 @@
 RES = 512
 LANES = 128
 TILE = 16
-WIDE = 8
+WIDE = 16
 STEPS = TILE // WIDE
 HALF = 64
 HIGH = 32
 BF16, F32 = jnp.bfloat16, jnp.float32
-
-
-def sigmoid(x):
-    return 0.5 * jnp.tanh(0.5 * x) + 0.5
 
 
 def norm(values, gain, shift):
@@ -38,14 +34,14 @@
     )
 
 
-def far_first(u, group):
+def far_first(by_core, group):
     def steps(offset):
         return offset // 32, offset // 8 % 4, offset // 2 % 4, offset % 2
 
     def hops(offset):
         return sum(min(v, 4 - v) for v in steps(offset)[:3])
 
-    members = [o for o in range(1, 128) if (steps(o)[3] if u == 0 else steps(o)[2] % 2) == 1 - group]
+    members = [o for o in range(1, 128) if (steps(o)[3] if by_core else steps(o)[2] % 2) == 1 - group]
     return sorted(members, key=lambda o: (-steps(o)[3], -hops(o)))
 
 
@@ -54,7 +50,7 @@
     pair, w_proj, w_gate, w_out, gain, shift,
     w_in_t, w_out_t, gain_t, shift_t, pair_t, gate_t, normed_t, left_f, right_f,
     send, recv, ssend, srecv, shared_m, shared_t, split_out, split_in,
-    send_sem, recv_sem, own_sem, ssend_sem, srecv_sem, sown_sem, in_sem, ready,
+    send_sem, recv_sem, ssend_sem, srecv_sem, in_sem, ready,
 ):
     devices = rows * cols
     row, col = lax.axis_index("row"), lax.axis_index("col")
@@ -98,14 +94,14 @@
     zs = [((((z + k) & 3) >> 1) * 2, (((z + k) & 3) & 1) * 4) for k in range(4)]
     cs = [core, 1 - core]
 
-    def everyone(u, group, start):
-        for offset in far_first(u, group):
+    def everyone(by_core, group, start):
+        for offset in far_first(by_core, group):
             dx, dy, dz, dc = offset // 32, offset // 8 % 4, offset // 2 % 4, offset % 2
             start(xs[dx] + zs[dz][0] + cs[dc], zs[dz][1] + ys[dy])
 
     def turn_in(u):
-        w_in_t[u, : 4 * C, :] = w_proj[u].astype(F32).T.astype(BF16)
-        w_in_t[u, 4 * C :, :] = w_gate[u].astype(F32).T.astype(BF16)
+        w_in_t[u, : 4 * C, :] = (0.5 * w_proj[u].astype(F32)).T.astype(BF16)
+        w_in_t[u, 4 * C :, :] = (0.5 * w_gate[u].astype(F32)).T.astype(BF16)
         gain_t[u, 0] = jnp.broadcast_to(gain[u, 0:1, :], (C, LANES)).T
         shift_t[u, 0] = jnp.broadcast_to(shift[u, 0:1, :], (C, LANES)).T
 
@@ -126,7 +122,7 @@
     def operand(u, side, n, normed):
         weights = w_in_t[u, side * 2 * C : (side + 1) * 2 * C]
         mixed = jnp.dot(weights, normed, preferred_element_type=F32)
-        product = sigmoid(mixed[:C]) * mixed[C:]
+        product = (jnp.tanh(mixed[:C]) + 1.0) * mixed[C:]
         for k in range(WIDE):
             target = (left_f, right_f)[side]
             target[pl.ds(n * WIDE + k, C, stride=TILE), :] = product[:, k * LANES : (k + 1) * LANES]
@@ -134,7 +130,7 @@
     def gates(u):
         def step(n, _):
             mixed = jnp.dot(w_in_t[u, 4 * C :], normed_t[n], preferred_element_type=F32)
-            gate_t[n] = sigmoid(mixed)
+            gate_t[n] = 0.5 * jnp.tanh(mixed) + 0.5
             return 0
 
         lax.fori_loop(0, STEPS, step, 0)
@@ -160,13 +156,9 @@
                     device_id=(r, q), device_id_type=MESH,
                 ).start()
 
-            everyone(u, group, start)
+            everyone(u == 0 or side == 0, group, start)
         if 1 in which:
-            own = pltpu.make_async_copy(
-                send.at[u, side, me], recv.at[u, side, me], own_sem.at[u, side]
-            )
-            own.start()
-            own.wait()
+            recv[u, side, me] = send[u, side, me]
 
     def gather(u, side, group, matrix):
         some = pl.ds(0, devices // 2 - group)
@@ -190,12 +182,10 @@
         def step_in(r, _):
             for m in range(cols // 4):
                 lanes = slice(m * LANES, (m + 1) * LANES)
-                if whole:
-                    lanes = pl.ds(pl.multiple_of((z_lo[group] * 2 + m) * LANES, LANES), LANES)
-                place(r * cols + z_lo[group] * 4 + 2 * m, (r,) if whole else (group, r), lanes)
-            return 0
-
-        if u == 0:
+                place(r * cols + z_lo[group] * 4 + 2 * m, (group, r), lanes)
+            return 0
+
+        if u == 0 or whole:
             lax.fori_loop(0, rows // 2, step_out, 0, unroll=4)
         else:
             lax.fori_loop(0, rows, step_in, 0, unroll=8)
@@ -226,12 +216,10 @@
                 device_id=(r, q), device_id_type=MESH,
             ).start()
 
-        everyone(u, group, start)
+        everyone(u == 0, group, start)
 
     def collect(u):
-        own = pltpu.make_async_copy(ssend.at[u, me], srecv.at[u, me], sown_sem.at[u])
-        own.start()
-        own.wait()
+        srecv[u, me] = ssend[u, me]
         some = pl.ds(0, devices - 1)
         pltpu.make_async_copy(srecv.at[u, some], srecv.at[u, some], srecv_sem.at[u]).wait()
         size = 8
@@ -264,10 +252,9 @@
         operand(0, 1, n, prepare(0, n, jnp.concatenate(blocks, axis=1)))
         return 0
 
-    lax.fori_loop(0, STEPS // 2, first_step, 0)
     pl.semaphore_wait(barrier, rows + cols - 2)
     greet_col(ready)
-    lax.fori_loop(STEPS // 2, STEPS, first_step, 0)
+    lax.fori_loop(0, STEPS, first_step, 0)
     pack(0, 1)
     pl.semaphore_wait(ready, cols - 1)
     ship(0, 1)
@@ -369,7 +356,7 @@
                 pltpu.VMEM((2, rows // 2, HIGH, RES), BF16),
                 pltpu.VMEM((2, rows, HIGH, RES // 2), BF16),
             ]
-            + [dma((2, 2)), dma((2, 2, 2)), dma((2, 2)), dma((2,)), dma((2,)), dma((2,)), dma((6,))]
+            + [dma((2, 2)), dma((2, 2, 2)), dma((2,)), dma((2,)), dma((6,))]
             + [pltpu.SemaphoreType.REGULAR],
             compiler_params=pltpu.CompilerParams(
                 collective_id=0, has_side_effects=True, vmem_limit_bytes=44 << 20

time: 59.7 us -> 58.9 us (0.987)
  Pallas kernels: 58.8 us -> 57.9 us
    pallas_call x1, Pallas kernels: 58.8 us -> 57.9 us  [body(): pl.pallas_call(functools.partial(kernel, rows, cols), out_shape=jax.Shape...]
where the time goes in v7:
time: 58.9 us; the launch traced here: 58.7 us
  Pallas kernels  57.9 us (98%)
  local copies, waits for them, and re-layouts  0.8 us (1%)
    pallas_call x1, Pallas kernels, body(): pl.pallas_call(functools.partial(kernel, rows, cols), out_shape=jax.Shape...  57.9 us

profile of v7, /device:TPU:1, one launch (start us, length us, event | category | flops | bytes accessed | tf_op | source)
XLA Modules:
  0.0 58.7 jit_solution(3009588596636389959)
XLA Ops:
  0.0 57.9 %shard_map.64 = bf16[32,64,128]{2,1,0:T(8,128)(2,1)S(1)} custom-call(bf16[32,64,128]{2,1,0:T(8,128)(2,1)} %pair_h.1, bf16[2,128,512]{2,1,0:T(8,128)(2,1)} %w_proj_h.1, bf16[2,128,128]{2,1,0:T(8,128)(2,1)} %w_gate_h.1, bf16[2,128,128]{2,1,0:T(8,128)(2,1)} %w_out_h.1, f32[2,2,128]{2,1,0:T(2,128)} %gain_h.1, f32[2,2,128]{2,1,0:T(2,128)} %shift_h.1), custom_call_target="tpu_custom_call" | custom-call | tf_op jit(solution)/shard_map/pallas_call | solution.py:334
  57.9 0.8 %copy.8 = bf16[32,64,128]{2,1,0:T(8,128)(2,1)} copy(bf16[32,64,128]{2,1,0:T(8,128)(2,1)S(1)} %shard_map.64) | data formatting | bytes 1048576

commit v8 on v7

--- a/solution.py
+++ b/solution.py
@@ -42,7 +42,11 @@
         return sum(min(v, 4 - v) for v in steps(offset)[:3])
 
     members = [o for o in range(1, 128) if (steps(o)[3] if by_core else steps(o)[2] % 2) == 1 - group]
-    return sorted(members, key=lambda o: (-steps(o)[3], -hops(o)))
+    def opposite(offset):
+        dx, dy, dz, dcore = steps(offset)
+        return (-dx % 4) * 32 + (-dy % 4) * 8 + (-dz % 4) * 2 + dcore
+
+    return sorted(members, key=lambda o: (-steps(o)[3], -hops(o), min(o, opposite(o)), o))
 
 
 def kernel(

time: 58.9 us -> 58.2 us (0.988)
  Pallas kernels: 57.9 us -> 57.2 us
    pallas_call x1, Pallas kernels: 57.9 us -> 57.2 us  [body(): pl.pallas_call(functools.partial(kernel, rows, cols), out_shape=jax.Shape...]
where the time goes in v8:
time: 58.2 us; the launch traced here: 58 us
  Pallas kernels  57.2 us (98%)
  local copies, waits for them, and re-layouts  0.8 us (1%)
    pallas_call x1, Pallas kernels, body(): pl.pallas_call(functools.partial(kernel, rows, cols), out_shape=jax.Shape...  57.2 us

profile of v8, /device:TPU:1, one launch (start us, length us, event | category | flops | bytes accessed | tf_op | source)
XLA Modules:
  0.0 58.0 jit_solution(957095719100555782)
XLA Ops:
  0.0 57.2 %shard_map.64 = bf16[32,64,128]{2,1,0:T(8,128)(2,1)S(1)} custom-call(bf16[32,64,128]{2,1,0:T(8,128)(2,1)} %pair_h.1, bf16[2,128,512]{2,1,0:T(8,128)(2,1)} %w_proj_h.1, bf16[2,128,128]{2,1,0:T(8,128)(2,1)} %w_gate_h.1, bf16[2,128,128]{2,1,0:T(8,128)(2,1)} %w_out_h.1, f32[2,2,128]{2,1,0:T(2,128)} %gain_h.1, f32[2,2,128]{2,1,0:T(2,128)} %shift_h.1), custom_call_target="tpu_custom_call" | custom-call | tf_op jit(solution)/shard_map/pallas_call | solution.py:338
  57.2 0.8 %copy.8 = bf16[32,64,128]{2,1,0:T(8,128)(2,1)} copy(bf16[32,64,128]{2,1,0:T(8,128)(2,1)S(1)} %shard_map.64) | data formatting | bytes 1048576

commit v9 on v8

--- a/solution.py
+++ b/solution.py
@@ -349,8 +349,8 @@
                 pltpu.VMEM((STEPS, C, WIDE * LANES), BF16),
                 pltpu.VMEM((STEPS, C, WIDE * LANES), F32),
                 pltpu.VMEM((STEPS, C, WIDE * LANES), BF16),
-                pltpu.VMEM((C * TILE, LANES), F32),
-                pltpu.VMEM((C * TILE, LANES), F32),
+                pltpu.VMEM((C * TILE + TILE, LANES), F32),
+                pltpu.VMEM((C * TILE + TILE, LANES), F32),
                 pltpu.VMEM((2, 2, devices, TILE, LANES), BF16),
                 pltpu.VMEM((2, 2, devices, TILE, LANES), BF16),
                 pltpu.VMEM((2, devices, TILE, LANES), BF16),

time: 58.2 us -> 58.1 us (level)
  no operation moved by 1% of the time
where the time goes in v9:
time: 58.1 us; the launch traced here: 58 us
  Pallas kernels  57.2 us (98%)
  local copies, waits for them, and re-layouts  0.8 us (1%)
    pallas_call x1, Pallas kernels, body(): pl.pallas_call(functools.partial(kernel, rows, cols), out_shape=jax.Shape...  57.2 us

profile of v9, /device:TPU:1, one launch (start us, length us, event | category | flops | bytes accessed | tf_op | source)
XLA Modules:
  0.0 58.0 jit_solution(2050459129269569793)
XLA Ops:
  0.0 57.2 %shard_map.64 = bf16[32,64,128]{2,1,0:T(8,128)(2,1)S(1)} custom-call(bf16[32,64,128]{2,1,0:T(8,128)(2,1)} %pair_h.1, bf16[2,128,512]{2,1,0:T(8,128)(2,1)} %w_proj_h.1, bf16[2,128,128]{2,1,0:T(8,128)(2,1)} %w_gate_h.1, bf16[2,128,128]{2,1,0:T(8,128)(2,1)} %w_out_h.1, f32[2,2,128]{2,1,0:T(2,128)} %gain_h.1, f32[2,2,128]{2,1,0:T(2,128)} %shift_h.1), custom_call_target="tpu_custom_call" | custom-call | tf_op jit(solution)/shard_map/pallas_call | solution.py:338
  57.2 0.8 %copy.8 = bf16[32,64,128]{2,1,0:T(8,128)(2,1)} copy(bf16[32,64,128]{2,1,0:T(8,128)(2,1)S(1)} %shard_map.64) | data formatting | bytes 1048576

commit v10 on v9

--- a/solution.py
+++ b/solution.py
@@ -93,9 +93,10 @@
     lax.fori_loop(1, rows, greet_row, 0)
     greet_col(barrier)
 
-    xs = [((x + k) & 3) * 4 for k in range(4)]
-    ys = [(y + k) & 3 for k in range(4)]
-    zs = [((((z + k) & 3) >> 1) * 2, (((z + k) & 3) & 1) * 4) for k in range(4)]
+    turn = [k - 2 * k * core for k in range(4)]
+    xs = [((x + turn[k]) & 3) * 4 for k in range(4)]
+    ys = [(y + turn[k]) & 3 for k in range(4)]
+    zs = [((((z + turn[k]) & 3) >> 1) * 2, (((z + turn[k]) & 3) & 1) * 4) for k in range(4)]
     cs = [core, 1 - core]
 
     def everyone(by_core, group, start):

time: 58.1 us -> 58.1 us (level)
  no operation moved by 1% of the time
where the time goes in v10:
time: 58.1 us; the launch traced here: 57.9 us
  Pallas kernels  57.1 us (98%)
  local copies, waits for them, and re-layouts  0.8 us (1%)
    pallas_call x1, Pallas kernels, body(): pl.pallas_call(functools.partial(kernel, rows, cols), out_shape=jax.Shape...  57.1 us

profile of v10, /device:TPU:1, one launch (start us, length us, event | category | flops | bytes accessed | tf_op | source)
XLA Modules:
  0.0 57.9 jit_solution(14251545714184246854)
XLA Ops:
  0.0 57.1 %shard_map.64 = bf16[32,64,128]{2,1,0:T(8,128)(2,1)S(1)} custom-call(bf16[32,64,128]{2,1,0:T(8,128)(2,1)} %pair_h.1, bf16[2,128,512]{2,1,0:T(8,128)(2,1)} %w_proj_h.1, bf16[2,128,128]{2,1,0:T(8,128)(2,1)} %w_gate_h.1, bf16[2,128,128]{2,1,0:T(8,128)(2,1)} %w_out_h.1, f32[2,2,128]{2,1,0:T(2,128)} %gain_h.1, f32[2,2,128]{2,1,0:T(2,128)} %shift_h.1), custom_call_target="tpu_custom_call" | custom-call | tf_op jit(solution)/shard_map/pallas_call | solution.py:339
  57.1 0.8 %copy.8 = bf16[32,64,128]{2,1,0:T(8,128)(2,1)} copy(bf16[32,64,128]{2,1,0:T(8,128)(2,1)S(1)} %shard_map.64) | data formatting | bytes 1048576
